TPU v7x, 256 devices: a whole 4x4x8 slice. The times are simulated.
256 devices in a mesh: gz: 64 (over x_lo, y, z), col: 4 (over x_hi, core).
Axes of the slice: x: 4 (x_hi: 2, x_lo: 2; x = x_hi * 2 + x_lo), y: 4, z: 8, core: 2. Of those that a mesh axis runs over, the one named last changes fastest.
Arguments:
- x_field: bfloat16 [64, 128, 1024], P('gz', 'col'), may hold values from -40 to 40
- weights: bfloat16 [256, 3456], P('col'), may hold values from -0.109375 to 0.109375
- grad_out: bfloat16 [64, 256, 1024], P('gz', 'col'), may hold values from -40 to 40
Outputs:
- y_field: bfloat16 [64, 256, 1024], P('gz', 'col')
- grad_input: bfloat16 [64, 128, 1024], P('gz', 'col')
- grad_weights: float32 [3456, 256], P('gz', 'col')
- patch_factor: float32 [3456, 3456], P('gz', 'col')
- grad_factor: float32 [256, 256], P('gz', 'col')
All inputs are finite; a program needn't handle non-finite values.
Results may differ from a plain program's by a relative error of at most 0.0008.
Values may be sent and summed in bfloat16 or wider, within the bound.
A program may use at most 384 MiB of HBM per device.

v0:
```python
import math

import jax
import jax.numpy as jnp
from jax import lax
from jax.sharding import PartitionSpec as P


def with_halo(block, sides, width):
    for axis, dim in sides:
        count = lax.axis_size(axis)
        forward = [(i, i + 1) for i in range(count - 1)]
        backward = [(target, source) for source, target in forward]
        low = lax.ppermute(
            lax.slice_in_dim(block, block.shape[dim] - width, None, axis=dim), axis, forward
        )
        high = lax.ppermute(lax.slice_in_dim(block, 0, width, axis=dim), axis, backward)
        block = jnp.concatenate([low, block, high], axis=dim)
    return block


def patch_columns(window, planes, side):
    pieces = []
    for a in range(3):
        for b in range(3):
            for e in range(3):
                pieces.append(window[a : a + planes, :, b : b + side, e : e + side])
    stacked = jnp.stack(pieces, axis=2)
    channels = stacked.shape[1]
    return jnp.transpose(stacked, (1, 2, 0, 3, 4)).reshape(channels * 27, planes * side * side)


def contract_cells(left, right):
    return lax.dot_general(
        left, right, (((1,), (1,)), ((), ())), preferred_element_type=jnp.float32
    )


def cells_last(field):
    return jnp.transpose(field, (1, 0, 2)).reshape(field.shape[1], -1)


def tap_sum(dy_ext, w_taps, planes, side):
    extent = dy_ext.shape[0]
    dy_pad = jnp.pad(
        dy_ext.reshape(extent, dy_ext.shape[1], side, side), ((0, 0), (0, 0), (1, 1), (1, 1))
    )
    acc = jnp.zeros((planes, w_taps.shape[1], side * side), jnp.float32)
    for a in range(3):
        for b in range(3):
            for e in range(3):
                tap = 9 * a + 3 * b + e
                part = dy_pad[2 - a : 2 - a + planes, :, 2 - b : 2 - b + side, 2 - e : 2 - e + side]
                part = part.reshape(planes, part.shape[1], side * side)
                acc = acc + jnp.einsum(
                    "oc,pos->pcs", w_taps[:, :, tap], part, preferred_element_type=jnp.float32
                )
    return acc


def shards(x_field, weights, grad_out):
    planes, in_local, cells = (x_field.shape[0], x_field.shape[1], x_field.shape[2])
    side = math.isqrt(cells)
    out_local = grad_out.shape[1]
    count_rows = planes * cells
    total = count_rows * lax.axis_size("gz")
    root_total = math.sqrt(total)
    kblock = in_local * 27
    x_ext = with_halo(x_field, (("gz", 0),), 1)
    x_all = lax.all_gather(x_ext, "col", axis=1, tiled=True)
    x_pad = jnp.pad(x_all.reshape(planes + 2, -1, side, side), ((0, 0), (0, 0), (1, 1), (1, 1)))
    patches = patch_columns(x_pad, planes, side)
    y_flat = jnp.dot(weights, patches, preferred_element_type=jnp.float32).astype(jnp.bfloat16)
    y_field = jnp.transpose(y_flat.reshape(out_local, planes, cells), (1, 0, 2))
    mine = lax.dynamic_slice_in_dim(patches, lax.axis_index("col") * kblock, kblock, 0)
    dy_cols = cells_last(grad_out)
    rows = patches
    patch_factor = lax.psum_scatter(
        contract_cells(rows, mine) / total, "gz", scatter_dimension=0, tiled=True
    )
    rows = patches
    grad_weights = lax.psum_scatter(
        contract_cells(rows, dy_cols) / root_total, "gz", scatter_dimension=0, tiled=True
    )
    dy_ext = with_halo(grad_out, (("gz", 0),), 1)
    w_taps = weights.reshape(out_local, -1, 27)
    partial_sum = tap_sum(dy_ext, w_taps, planes, side)
    grad_input = lax.psum_scatter(partial_sum, "col", scatter_dimension=1, tiled=True).astype(
        jnp.bfloat16
    )
    dy_full = cells_last(lax.all_gather(grad_out, "col", axis=1, tiled=True))
    gram_part = contract_cells(dy_full, dy_cols) / total
    grad_factor = lax.psum_scatter(gram_part, "gz", scatter_dimension=0, tiled=True)
    return (y_field, grad_input, grad_weights, patch_factor, grad_factor)


def solution(mesh):
    return jax.shard_map(
        shards,
        mesh=mesh,
        in_specs=(P("gz", "col", None), P("col", None), P("gz", "col", None)),
        out_specs=(
            P("gz", "col", None),
            P("gz", "col", None),
            P("gz", "col"),
            P("gz", "col"),
            P("gz", "col"),
        ),
        check_vma=False,
    )
```

profile of v0, /device:TPU:1, one launch (start us, length us, event | category | flops | bytes accessed | tf_op | source)
XLA Modules:
  0.0 708.2 jit_solution(6062400482681170816)
XLA Ops:
  7.2 4.4 collective-permute-start
  11.6 1.3 collective-permute-start.1
  12.9 9.7 %all_gather.7 = bf16[1,256,1024]{2,1,0:T(8,128)(2,1)S(1)} all-gather(bf16[1,64,1024]{2,1,0:T(8,128)(2,1)} %param.5), channel_id=1, replica_groups=mesh['gz'=64,'col'=4] {'col'}, dimensions={1}, use_global_device_ids=true | all-gather | bytes 655360 | tf_op jit(solution)/shard_map/all_gather | solution.py:91
  22.6 1.8 convolution_multiply_fusion.2
  24.5 1.4 copy.53
  26.2 2.0 fusion.103
  28.2 10.2 %all_gather.6 = bf16[3,128,1024]{2,1,0:T(8,128)(2,1)S(1)} all-gather(bf16[3,32,1024]{2,1,0:T(8,128)(2,1)S(1)} %pad_maximum_fusion.1), channel_id=1, replica_groups=mesh['gz'=64,'col'=4] {'col'}, dimensions={1}, use_global_device_ids=true | all-gather | bytes 983040 | tf_op jit(solution)/shard_map/all_gather | solution.py:70
  40.4 0.8 fusion.24
  41.2 0.8 fusion.26
  42.7 0.8 fusion.28
  48.0 0.8 fusion.42
  51.8 0.8 fusion.50
  54.8 0.8 fusion.58
  56.3 0.8 fusion.60
  58.6 0.8 fusion.66
  59.4 37.5 %copy.49 = bf16[1,128,27,32,32]{4,3,2,1,0:T(8,128)(2,1)} copy(bf16[1,128,27,32,32]{1,4,3,2,0:T(8,128)(2,1)} %fusion.66) | data formatting | bytes 14155776 | tf_op jit(solution)/shard_map/stack | solution.py:28
  96.9 38.2 %reshape_transpose.7 = bf16[3456,1024]{1,0:T(8,128)(2,1)} reshape(bf16[1,128,27,32,32]{4,3,2,1,0:T(8,128)(2,1)} %copy.49) | data formatting | bytes 14155776 | tf_op jit(solution)/shard_map/reshape;transpose | solution.py:30
  135.2 5.1 convolution_multiply_fusion.1
  140.3 10.0 %convolution_multiply_fusion = f32[3456,864]{1,0:T(8,128)} fusion(bf16[3456,1024]{1,0:T(8,128)(2,1)S(1)} %copy-done, s32[]{:T(128)S(6)} %select_n.3), kind=kOutput, calls=%fused_computation | convolution fusion | flops 6118281216 | bytes 20791300 | tf_op jit(solution)/shard_map/dot_general | solution.py:34
  150.3 190.6 %fusion.102 = (f32[64,64]{1,0:T(8,128)S(1)}, f32[64,864]{1,0:T(8,128)S(1)}) fusion(f32[3456,64]{1,0:T(8,128)S(1)} %convolution_multiply_fusion.1, f32[3456,864]{1,0:T(8,128)} %convolution_multiply_fusion), kind=kCustom, calls=%all-reduce-scatter.2 | all-reduce-scatter fusion | flops 3801089 | bytes 13067264
  341.0 4.8 collective-permute-start.10
  345.7 5.0 collective-permute-start.13
  352.2 1.0 copy.62
  353.2 0.9 copy.63
  354.1 0.9 copy.64
  355.1 0.9 copy.65
  356.0 0.9 copy.66
  356.9 0.9 copy.67
  357.9 0.9 copy.68
  358.8 0.9 copy.69
  359.8 0.9 copy.75
  360.7 0.9 copy.74
  361.7 0.9 copy.73
  362.6 0.9 copy.72
  363.6 0.9 copy.71
  364.5 0.9 copy.70
  369.1 2.6 collective-permute-start.11
  371.7 2.6 collective-permute-start.12
  374.3 3.9 collective-permute-start.4
  378.3 2.2 collective-permute-start.5
  380.5 6.5 collective-permute-start.6
  387.0 5.2 fusion.17
  392.1 4.1 collective-permute-start.2
  396.3 1.3 collective-permute-start.3
  397.6 7.0 collective-permute-start.7
  404.6 2.2 collective-permute-start.8
  406.9 6.2 collective-permute-start.9
  413.0 119.3 %all-reduce.12.cloned.1.call-done = f32[256,64]{1,0:T(8,128)} async-done(((f32[256,64]{1,0:T(8,128)}), f32[256,64]{1,0:T(8,128)}) %all-reduce.12.cloned.1.call-update) | async-done | bytes 65552
  532.3 1.3 constant_dynamic-slice_fusion.2
  533.6 3.3 collective-permute-start.14
  536.9 2.0 collective-permute-start.15
  538.8 1.8 collective-permute-start.16
  540.7 1.7 concatenate.8
  543.0 1.6 collective-permute-start.17
  544.6 2.0 collective-permute-start.23
  546.8 1.1 pad_slice_fusion.9
  554.4 6.7 collective-permute-done.23
  561.1 1.3 collective-permute-start.18
  562.4 9.8 %collective-permute-start.19 = (f32[64,864]{1,0:T(8,128)S(1)}, f32[64,864]{1,0:T(8,128)S(1)}, u32[]{:S(2)}, u32[]{:S(2)}) collective-permute-start(f32[64,864]{1,0:T(8,128)S(1)} %get-tuple-element.23), channel_id=1, source_target_pairs={{0,24},{4,28},{8,32},{12,36},{16,40},{20,44},{24,48},{28,52},{32,5... | collective-permute-start | bytes 663560
  572.3 1.7 collective-permute-start.20
  574.0 5.0 collective-permute-start.21
  579.0 4.1 collective-permute-start.22
  583.1 106.2 %all-reduce.13 = bf16[1,128,1024]{2,0,1:T(2,128)(2,1)S(1)} all-reduce(f32[1,128,1024]{2,0,1:T(1,128)S(1)} %copy.81), channel_id=2, replica_groups=mesh['gz'=64,'col'=4] {'col'}, use_global_device_ids=true, to_apply=%region_0.1.clone | all-reduce | flops 131072 | bytes 786432
  691.7 8.9 %concatenate.9 = f32[694,864]{1,0:T(8,128)S(1)} concatenate(f32[54,864]{1,0:T(8,128)} %copy-done.8, f32[64,864]{1,0:T(8,128)} %collective-permute-done.22, f32[64,864]{1,0:T(8,128)} %copy-done.7, f32[64,864]{1,0:T(8,128)} %copy-done.6, f32[64,864]{1,0:T(8,128)} %copy-done.5, f32[64,864]{1,0:T(8,128)} %copy-done.4, f32[64,864]{1,0:T(8,128)} %copy-done.3, f32[64,864]{1,0:T(8,128)} %copy-done.2, ...), dimensions={0} | concatenate | bytes 4796928
  (125 shorter events, 28.2 us)
Async XLA Ops:
  7.2 21.0 %copy-start.9 = (bf16[1,32,1024]{2,1,0:T(8,128)(2,1)S(1)}, bf16[1,32,1024]{2,1,0:T(8,128)(2,1)}, u32[]{:S(2)}) copy-start(bf16[1,32,1024]{2,1,0:T(8,128)(2,1)} %param.3) | copy-start | bytes 196612
  7.2 525.1 %all-reduce.12.cloned.1.call-start = ((), (), s32[]{:S(2)}) async-start(), calls=%async_computation | async-start | bytes 262144
  7.2 21.0 %collective-permute-start = (bf16[1,32,1024]{2,1,0:T(8,128)(2,1)}, bf16[1,32,1024]{2,1,0:T(8,128)(2,1)S(1)}, u32[]{:S(2)}, u32[]{:S(2)}) collective-permute-start(bf16[1,32,1024]{2,1,0:T(8,128)(2,1)} %param.3), channel_id=1, source_target_pairs={{0,4},{4,8},{8,12},{12,16},{16,20},{20,24},{24,28},{28,32},{32,36}... | collective-permute-start | bytes 196616 | tf_op jit(solution)/shard_map/ppermute | solution.py:14
  11.6 16.6 %collective-permute-start.1 = (bf16[1,32,1024]{2,1,0:T(8,128)(2,1)}, bf16[1,32,1024]{2,1,0:T(8,128)(2,1)S(1)}, u32[]{:S(2)}, u32[]{:S(2)}) collective-permute-start(bf16[1,32,1024]{2,1,0:T(8,128)(2,1)} %param.3), channel_id=1, source_target_pairs={{4,0},{8,4},{12,8},{16,12},{20,16},{24,20},{28,24},{32,28},{36,32}... | collective-permute-start | bytes 196616 | tf_op jit(solution)/shard_map/ppermute | solution.py:17
  96.9 38.2 %copy-start.1 = (bf16[1,64,1024]{2,1,0:T(8,128)(2,1)S(1)}, bf16[1,64,1024]{2,1,0:T(8,128)(2,1)}, u32[]{:S(2)}) copy-start(bf16[1,64,1024]{2,1,0:T(8,128)(2,1)} %param.5) | copy-start | bytes 393220
  135.2 5.2 copy-start
  150.3 215.6 %copy-start.11 = (u32[256]{0:T(256)S(1)}, u32[256]{0:T(256)}, u32[]{:S(2)}) copy-start(u32[256]{0:T(256)} %constant.28) | copy-start | bytes 3076
  150.3 216.2 %copy-start.10 = (u32[256]{0:T(256)S(1)}, u32[256]{0:T(256)}, u32[]{:S(2)}) copy-start(u32[256]{0:T(256)} %constant.32) | copy-start | bytes 3076
  341.0 39.5 %collective-permute-start.10 = (f32[64,64]{1,0:T(8,128)S(1)}, f32[64,64]{1,0:T(8,128)S(1)}, u32[]{:S(2)}, u32[]{:S(2)}) collective-permute-start(f32[64,64]{1,0:T(8,128)S(1)} %get-tuple-element.22), channel_id=1, source_target_pairs={{0,28},{4,32},{8,36},{12,40},{16,44},{20,48},{24,52},{28,56},{32,6... | collective-permute-start | bytes 49160
  345.7 32.5 %collective-permute-start.13 = (f32[54,64]{1,0:T(8,128)S(1)}, f32[54,64]{1,0:T(8,128)S(1)}, u32[]{:S(2)}, u32[]{:S(2)}) collective-permute-start(f32[54,64]{1,0:T(8,128)S(1)} %slice.357), channel_id=1, source_target_pairs={{0,40},{4,44},{8,48},{12,52},{16,56},{20,60},{24,64},{28,68},{32,7... | collective-permute-start | bytes 41480
  369.1 23.0 %collective-permute-start.11 = (f32[64,64]{1,0:T(8,128)S(1)}, f32[64,64]{1,0:T(8,128)S(1)}, u32[]{:S(2)}, u32[]{:S(2)}) collective-permute-start(f32[64,64]{1,0:T(8,128)S(1)} %get-tuple-element.22), channel_id=1, source_target_pairs={{0,32},{4,36},{8,40},{12,44},{16,48},{20,52},{24,56},{28,60},{32,6... | collective-permute-start | bytes 49160
  371.7 24.6 %collective-permute-start.12 = (f32[64,64]{1,0:T(8,128)S(1)}, f32[64,64]{1,0:T(8,128)S(1)}, u32[]{:S(2)}, u32[]{:S(2)}) collective-permute-start(f32[64,64]{1,0:T(8,128)S(1)} %get-tuple-element.22), channel_id=1, source_target_pairs={{0,36},{4,40},{8,44},{12,48},{16,52},{20,56},{24,60},{28,64},{32,6... | collective-permute-start | bytes 49160
  374.3 23.3 %collective-permute-start.4 = (f32[64,64]{1,0:T(8,128)S(1)}, f32[64,64]{1,0:T(8,128)S(1)}, u32[]{:S(2)}, u32[]{:S(2)}) collective-permute-start(f32[64,64]{1,0:T(8,128)S(1)} %get-tuple-element.22), channel_id=1, source_target_pairs={{0,4},{4,8},{8,12},{12,16},{16,20},{20,24},{24,28},{28,32},{32,36}... | collective-permute-start | bytes 49160
  378.3 26.4 %collective-permute-start.5 = (f32[64,64]{1,0:T(8,128)S(1)}, f32[64,64]{1,0:T(8,128)S(1)}, u32[]{:S(2)}, u32[]{:S(2)}) collective-permute-start(f32[64,64]{1,0:T(8,128)S(1)} %get-tuple-element.22), channel_id=1, source_target_pairs={{0,8},{4,12},{8,16},{12,20},{16,24},{20,28},{24,32},{28,36},{32,40... | collective-permute-start | bytes 49160
  380.5 26.4 %collective-permute-start.6 = (f32[64,64]{1,0:T(8,128)S(1)}, f32[64,64]{1,0:T(8,128)S(1)}, u32[]{:S(2)}, u32[]{:S(2)}) collective-permute-start(f32[64,64]{1,0:T(8,128)S(1)} %get-tuple-element.22), channel_id=1, source_target_pairs={{0,12},{4,16},{8,20},{12,24},{16,28},{20,32},{24,36},{28,40},{32,4... | collective-permute-start | bytes 49160
  392.1 150.9 %collective-permute-start.2 = (bf16[1,64,1024]{1,2,0:T(8,128)(2,1)S(1)}, bf16[1,64,1024]{1,2,0:T(8,128)(2,1)S(1)}, u32[]{:S(2)}, u32[]{:S(2)}) collective-permute-start(bf16[1,64,1024]{1,2,0:T(8,128)(2,1)S(1)} %copy.50), channel_id=1, source_target_pairs={{0,4},{4,8},{8,12},{12,16},{16,20},{20,24},{24,28},{28,32},{32,36}... | collective-permute-start | bytes 393224 | tf_op jit(solution)/shard_map/ppermute | solution.py:14
  396.3 148.3 %collective-permute-start.3 = (bf16[1,64,1024]{1,2,0:T(8,128)(2,1)S(1)}, bf16[1,64,1024]{1,2,0:T(8,128)(2,1)S(1)}, u32[]{:S(2)}, u32[]{:S(2)}) collective-permute-start(bf16[1,64,1024]{1,2,0:T(8,128)(2,1)S(1)} %copy.50), channel_id=1, source_target_pairs={{4,0},{8,4},{12,8},{16,12},{20,16},{24,20},{28,24},{32,28},{36,32}... | collective-permute-start | bytes 393224 | tf_op jit(solution)/shard_map/ppermute | solution.py:17
  397.6 136.0 %collective-permute-start.7 = (f32[64,64]{1,0:T(8,128)S(1)}, f32[64,64]{1,0:T(8,128)S(1)}, u32[]{:S(2)}, u32[]{:S(2)}) collective-permute-start(f32[64,64]{1,0:T(8,128)S(1)} %get-tuple-element.22), channel_id=1, source_target_pairs={{0,16},{4,20},{8,24},{12,28},{16,32},{20,36},{24,40},{28,44},{32,4... | collective-permute-start | bytes 49160
  404.6 132.2 %collective-permute-start.8 = (f32[64,64]{1,0:T(8,128)S(1)}, f32[64,64]{1,0:T(8,128)S(1)}, u32[]{:S(2)}, u32[]{:S(2)}) collective-permute-start(f32[64,64]{1,0:T(8,128)S(1)} %get-tuple-element.22), channel_id=1, source_target_pairs={{0,20},{4,24},{8,28},{12,32},{16,36},{20,40},{24,44},{28,48},{32,5... | collective-permute-start | bytes 49160
  406.9 132.0 %collective-permute-start.9 = (f32[64,64]{1,0:T(8,128)S(1)}, f32[64,64]{1,0:T(8,128)S(1)}, u32[]{:S(2)}, u32[]{:S(2)}) collective-permute-start(f32[64,64]{1,0:T(8,128)S(1)} %get-tuple-element.22), channel_id=1, source_target_pairs={{0,24},{4,28},{8,32},{12,36},{16,40},{20,44},{24,48},{28,52},{32,5... | collective-permute-start | bytes 49160
  533.6 28.8 %collective-permute-start.14 = (f32[64,864]{1,0:T(8,128)S(1)}, f32[64,864]{1,0:T(8,128)S(1)}, u32[]{:S(2)}, u32[]{:S(2)}) collective-permute-start(f32[64,864]{1,0:T(8,128)S(1)} %get-tuple-element.23), channel_id=1, source_target_pairs={{0,4},{4,8},{8,12},{12,16},{16,20},{20,24},{24,28},{28,32},{32,36}... | collective-permute-start | bytes 663560
  536.9 35.4 %collective-permute-start.15 = (f32[64,864]{1,0:T(8,128)S(1)}, f32[64,864]{1,0:T(8,128)S(1)}, u32[]{:S(2)}, u32[]{:S(2)}) collective-permute-start(f32[64,864]{1,0:T(8,128)S(1)} %get-tuple-element.23), channel_id=1, source_target_pairs={{0,8},{4,12},{8,16},{12,20},{16,24},{20,28},{24,32},{28,36},{32,40... | collective-permute-start | bytes 663560
  538.8 35.2 %collective-permute-start.16 = (f32[64,864]{1,0:T(8,128)S(1)}, f32[64,864]{1,0:T(8,128)S(1)}, u32[]{:S(2)}, u32[]{:S(2)}) collective-permute-start(f32[64,864]{1,0:T(8,128)S(1)} %get-tuple-element.23), channel_id=1, source_target_pairs={{0,12},{4,16},{8,20},{12,24},{16,28},{20,32},{24,36},{28,40},{32,4... | collective-permute-start | bytes 663560
  543.0 36.0 %collective-permute-start.17 = (f32[64,864]{1,0:T(8,128)S(1)}, f32[64,864]{1,0:T(8,128)S(1)}, u32[]{:S(2)}, u32[]{:S(2)}) collective-permute-start(f32[64,864]{1,0:T(8,128)S(1)} %get-tuple-element.23), channel_id=1, source_target_pairs={{0,16},{4,20},{8,24},{12,28},{16,32},{20,36},{24,40},{28,44},{32,4... | collective-permute-start | bytes 663560
  544.6 16.5 %collective-permute-start.23 = (f32[54,864]{1,0:T(8,128)S(1)}, f32[54,864]{1,0:T(8,128)S(1)}, u32[]{:S(2)}, u32[]{:S(2)}) collective-permute-start(f32[54,864]{1,0:T(8,128)S(1)} %slice.358), channel_id=1, source_target_pairs={{0,40},{4,44},{8,48},{12,52},{16,56},{20,60},{24,64},{28,68},{32,7... | collective-permute-start | bytes 559880
  561.1 1.3 copy-start.8
  561.1 129.1 %collective-permute-start.18 = (f32[64,864]{1,0:T(8,128)S(1)}, f32[64,864]{1,0:T(8,128)S(1)}, u32[]{:S(2)}, u32[]{:S(2)}) collective-permute-start(f32[64,864]{1,0:T(8,128)S(1)} %get-tuple-element.23), channel_id=1, source_target_pairs={{0,20},{4,24},{8,28},{12,32},{16,36},{20,40},{24,44},{28,48},{32,5... | collective-permute-start | bytes 663560
  562.4 127.7 %collective-permute-start.19 = (f32[64,864]{1,0:T(8,128)S(1)}, f32[64,864]{1,0:T(8,128)S(1)}, u32[]{:S(2)}, u32[]{:S(2)}) collective-permute-start(f32[64,864]{1,0:T(8,128)S(1)} %get-tuple-element.23), channel_id=1, source_target_pairs={{0,24},{4,28},{8,32},{12,36},{16,40},{20,44},{24,48},{28,52},{32,5... | collective-permute-start | bytes 663560
  572.3 117.9 %collective-permute-start.20 = (f32[64,864]{1,0:T(8,128)S(1)}, f32[64,864]{1,0:T(8,128)S(1)}, u32[]{:S(2)}, u32[]{:S(2)}) collective-permute-start(f32[64,864]{1,0:T(8,128)S(1)} %get-tuple-element.23), channel_id=1, source_target_pairs={{0,28},{4,32},{8,36},{12,40},{16,44},{20,48},{24,52},{28,56},{32,6... | collective-permute-start | bytes 663560
  574.0 116.2 %copy-start.2 = (f32[64,864]{1,0:T(8,128)}, f32[64,864]{1,0:T(8,128)S(1)}, u32[]{:S(2)}) copy-start(f32[64,864]{1,0:T(8,128)S(1)} %collective-permute-done.16) | copy-start | bytes 663556
  574.0 116.2 %collective-permute-start.21 = (f32[64,864]{1,0:T(8,128)S(1)}, f32[64,864]{1,0:T(8,128)S(1)}, u32[]{:S(2)}, u32[]{:S(2)}) collective-permute-start(f32[64,864]{1,0:T(8,128)S(1)} %get-tuple-element.23), channel_id=1, source_target_pairs={{0,32},{4,36},{8,40},{12,44},{16,48},{20,52},{24,56},{28,60},{32,6... | collective-permute-start | bytes 663560
  579.0 111.2 %copy-start.3 = (f32[64,864]{1,0:T(8,128)}, f32[64,864]{1,0:T(8,128)S(1)}, u32[]{:S(2)}) copy-start(f32[64,864]{1,0:T(8,128)S(1)} %collective-permute-done.17) | copy-start | bytes 663556
  579.0 112.7 %collective-permute-start.22 = (f32[64,864]{1,0:T(8,128)S(1)}, f32[64,864]{1,0:T(8,128)}, u32[]{:S(2)}, u32[]{:S(2)}) collective-permute-start(f32[64,864]{1,0:T(8,128)S(1)} %get-tuple-element.23), channel_id=1, source_target_pairs={{0,36},{4,40},{8,44},{12,48},{16,52},{20,56},{24,60},{28,64},{32,6... | collective-permute-start | bytes 663560
  690.2 0.7 copy-start.4
  690.2 0.8 copy-start.5
  690.2 0.8 copy-start.6
  691.0 0.7 copy-start.7
Sparse Core Ops, SparseCore 0:
  24.6 507.6 all-reduce.11
where the time goes:
time: 713 us; the launch traced here: 708 us
  blocking collectives  317 us (44%)
  local copies, waits for them, and re-layouts  134 us (19%)
  waiting for transfers between devices  126 us (18%)
  starting transfers between devices  86.6 us (12%)
  matrix products  27.8 us (4%)
  between operations  16.9 us (2%)
    unnamed x2, blocking collectives  297 us
    unnamed x22, waiting for transfers between devices  126 us
    unnamed x21, starting transfers between devices  75.5 us
    another operation x2, local copies, waits for them, and re-layouts, patch_columns(): stacked = jnp.stack(pieces, axis=2)  38.3 us
    another operation x1, local copies, waits for them, and re-layouts, patch_columns(): jnp.transpose(stacked, (1, 2, 0, 3, 4))  38.2 us
    unnamed x62, local copies, waits for them, and re-layouts  37.8 us
    dot_general x3, matrix products, contract_cells(): lax.dot_general(left, right, (((1,), (1,)), ((), ())), preferred_element_...  17 us
    slice x29, local copies, waits for them, and re-layouts, tap_sum(): w_taps[:, :, tap]  16.9 us
  transfers between devices with their start and end apart: 25, of which 2 were waited for; matrix products, arithmetic and copies ran while one was open for 48% of the time, Pallas kernels for 0%

commit v1 on v0

v1 whole, which is shorter than its diff:
```python
import jax
import jax.numpy as jnp
import numpy as np
from jax import lax
from jax.experimental import pallas as pl
from jax.experimental.pallas import tpu as pltpu
from jax.sharding import PartitionSpec as P

MESH = pl.DeviceIdType.MESH
BF, F32 = jnp.bfloat16, jnp.float32
SIDE, YX, TAPS = 32, 1024, 27
NT = (((1,), (1,)), ((), ()))


def kind(first, second):
    if first != second:
        return second - first + 2
    return {1: 2, 2: 5, 0: 6}[first]


def channel_order():
    out = np.zeros((128, 128), np.float32)
    for zi in range(8):
        for k in range(8):
            for p in range(2):
                out[zi * 16 + 2 * k + p, 16 * k + 2 * zi + p] = 1
    return out


def type_choice():
    out = np.zeros((144, 49), np.float32)
    for b2 in range(3):
        for e2 in range(3):
            for b in range(3):
                for e in range(3):
                    out[(b2 * 3 + e2) * 16 + b * 3 + e, kind(b, b2) * 7 + kind(e, e2)] = 1
    return out


def column_order():
    out = np.zeros((1152, 864), np.float32)
    for be in range(9):
        for a in range(3):
            for c in range(32):
                out[be * 128 + a * 32 + c, c * 27 + a * 9 + be] = 1
    return out


def moved(value, step):
    step = step % YX
    return value if step == 0 else pltpu.roll(value, shift=(YX - step) % YX, axis=1)


def cell_masks():
    cell = lax.broadcasted_iota(jnp.int32, (1, YX), 1)
    return cell // SIDE, cell % SIDE


def keep(where):
    return where.astype(F32).astype(BF)


def kernel(x_ref, g_ref, wy_ref, wg_ref, order_ref, choice_ref, column_ref,
           y_ref, gi_ref, gw_ref, pf_ref, gf_ref,
           xc, gc, gh, sp, rp, xr, xp, gp, rv, da, db, mg, rg, b3, rb, mp, rpf, gi, rgi, up, lh,
           send_sem, late_sem, xc_sem, gc_sem, gh_sem, sp_sem, rp_sem, rg_sem, rb_sem, rpf_sem, gi_sem):
    gz, col = lax.axis_index("gz"), lax.axis_index("col")
    k, z = gz // 8, gz % 8
    core = col + 1 - 2 * (col % 2)
    far = (col + 2) % 4
    diag = (core + 2) % 4
    above, below = (gz + 1) % 64, (gz + 63) % 64
    ring = [(z + j) % 8 for j in range(1, 8)]
    peers = [(k + j) % 8 for j in range(1, 8)]
    skip = jnp.where(z == 6, (gz + 3) % 64, (gz + 61) % 64)
    has_skip = jnp.logical_or(z == 1, z == 6)

    sends = []

    def send(src, dst, sem, target):
        copy = pltpu.make_async_remote_copy(
            src_ref=src, dst_ref=dst, send_sem=send_sem.at[len(sends)], recv_sem=sem,
            device_id=target, device_id_type=MESH)
        copy.start()
        sends.append(copy)

    def arrived(dst, sem):
        pltpu.make_async_remote_copy(
            src_ref=dst, dst_ref=dst, send_sem=send_sem.at[0], recv_sem=sem,
            device_id=(gz, core), device_id_type=MESH).wait_recv()

    barrier = pltpu.get_barrier_semaphore()
    partners = [(gz, core), (gz, far), (above, col), (below, col)]
    partners += [(k * 8 + zj, col) for zj in ring] + [(kj * 8 + z, col) for kj in peers]
    for target in partners:
        pl.semaphore_signal(barrier, inc=1, device_id=target, device_id_type=MESH)

    @pl.when(has_skip)
    def _():
        pl.semaphore_signal(barrier, inc=1, device_id=(skip, col), device_id_type=MESH)

    pl.semaphore_wait(barrier, len(partners) + jnp.where(has_skip, 1, 0))

    send(x_ref, xc.at[col, 1], xc_sem.at[col, 1], (gz, far))
    send(x_ref, xc.at[col, 1], xc_sem.at[col, 1], (gz, core))
    send(g_ref, gh.at[0], gh_sem.at[0], (above, col))
    send(g_ref, gh.at[1], gh_sem.at[1], (below, col))
    send(x_ref, xc.at[col, 0], xc_sem.at[col, 0], (above, col))
    send(x_ref, xc.at[col, 2], xc_sem.at[col, 2], (below, col))
    skip_out = jnp.where(z == 6, 0, 11)
    skip_in = jnp.where(z == 6, 11, 0)

    def skip_copy():
        return pltpu.make_async_remote_copy(
            src_ref=x_ref, dst_ref=sp.at[skip_out], send_sem=late_sem.at[0], recv_sem=sp_sem.at[skip_out],
            device_id=(skip, col), device_id_type=MESH)

    @pl.when(has_skip)
    def _():
        skip_copy().start()

    send(g_ref, gc.at[col], gc_sem.at[col], (gz, far))
    send(g_ref, gc.at[col], gc_sem.at[col], (gz, core))
    for zj in ring:
        send(x_ref, sp.at[2 + z], sp_sem.at[2 + z], (k * 8 + zj, col))
    xc[col, 1] = x_ref[...]
    gc[col] = g_ref[...]
    sp[2 + z] = x_ref[...]

    arrived(xc.at[far, 1], xc_sem.at[far, 1])
    send(xc.at[far, 1], xc.at[far, 1], xc_sem.at[far, 1], (gz, core))
    arrived(xc.at[core, 1], xc_sem.at[core, 1])
    arrived(xc.at[diag, 1], xc_sem.at[diag, 1])
    x_all = xc[:, 1].reshape(128, YX)
    xr[...] = jnp.dot(order_ref[...], x_all, preferred_element_type=F32).astype(BF).reshape(8, 16, YX)
    for zj in ring:
        send(xr.at[zj], rp.at[z], rp_sem.at[z], (k * 8 + zj, col))
    rp[z] = xr[z]

    for side, edge in ((0, 0), (2, 63)):
        arrived(xc.at[col, side], xc_sem.at[col, side])

        @pl.when(gz == edge)
        def _():
            xc[col, side] = jnp.zeros((32, YX), BF)

        send(xc.at[col, side], xc.at[col, side], xc_sem.at[col, side], (gz, far))
        send(xc.at[col, side], xc.at[col, side], xc_sem.at[col, side], (gz, core))

    @pl.when(has_skip)
    def _():
        arrived(sp.at[skip_in], sp_sem.at[skip_in])

    @pl.when(jnp.logical_and(z == 1, k == 0))
    def _():
        sp[0] = jnp.zeros((32, YX), BF)

    @pl.when(jnp.logical_and(z == 6, k == 7))
    def _():
        sp[11] = jnp.zeros((32, YX), BF)

    forwards = ((1, 0, lambda: sp.at[0]), (0, 1, lambda: xc.at[col, 0]),
                (7, 10, lambda: xc.at[col, 2]), (6, 11, lambda: sp.at[11]))

    def forward_copies(owner, slot, source):
        return [pltpu.make_async_remote_copy(
            src_ref=source(), dst_ref=sp.at[slot], send_sem=late_sem.at[1 + j], recv_sem=sp_sem.at[slot],
            device_id=(k * 8 + (owner + 1 + j) % 8, col), device_id_type=MESH) for j in range(7)]

    for owner, slot, source in forwards:
        @pl.when(z == owner)
        def _():
            for copy in forward_copies(owner, slot, source):
                copy.start()

    @pl.when(z == 0)
    def _():
        sp[1] = xc[col, 0]

    @pl.when(z == 7)
    def _():
        sp[10] = xc[col, 2]

    arrived(gc.at[far], gc_sem.at[far])
    send(gc.at[far], gc.at[far], gc_sem.at[far], (gz, core))

    row, place = cell_masks()
    in_row = {-1: keep(place >= 1), 1: keep(place < SIDE - 1)}
    in_plane = {-1: keep(row >= 1), 1: keep(row < SIDE - 1)}

    def shifted(value, dy, dx):
        if dx:
            value = moved(value, dx) * in_row[dx]
        if dy:
            value = moved(value, SIDE * dy) * in_plane[dy]
        return value

    for slot, edge in ((0, 0), (1, 63)):
        arrived(gh.at[slot], gh_sem.at[slot])

        @pl.when(gz == edge)
        def _():
            gh[slot] = jnp.zeros((64, YX), BF)

    for a in range(3):
        plane = (gh[1], g_ref[...], gh[0])[a]
        for e in range(3):
            line = shifted(plane, 0, 1 - e)
            for b in range(3):
                tap = 9 * a + 3 * b + e
                gp[tap * 64:(tap + 1) * 64, :] = shifted(line, 1 - b, 0)

    x_all = xc[:, 1].reshape(128, YX)
    grad_w = lax.dot_general(x_all, gp[...], NT, preferred_element_type=F32)
    for kj in range(8):
        mg[kj, :, 0:1728] = grad_w[16 * kj:16 * kj + 16]
        mg[kj, :, 1728:1792] = jnp.zeros((16, 64), F32)
    arrived(gc.at[core], gc_sem.at[core])
    arrived(gc.at[diag], gc_sem.at[diag])
    gram = lax.dot_general(gc[...].reshape(256, YX), g_ref[...], NT, preferred_element_type=F32)
    for kj in range(8):
        mg[kj, :, 1792:1856] = gram[32 * kj:32 * kj + 16]
        mg[kj, :, 1856:1920] = gram[32 * kj + 16:32 * kj + 32]
    for kj in peers:
        send(mg.at[kj], rg.at[k], rg_sem.at[k], (kj * 8 + z, col))

    gi[...] = jnp.dot(wg_ref[...], gp[...], preferred_element_type=F32).reshape(4, 32, YX)
    send(gi.at[core], rgi.at[0], gi_sem.at[0], (gz, core))
    send(gi.at[diag], rgi.at[1], gi_sem.at[1], (gz, core))

    for side in (0, 2):
        arrived(xc.at[far, side], xc_sem.at[far, side])
        send(xc.at[far, side], xc.at[far, side], xc_sem.at[far, side], (gz, core))
    arrived(rgi.at[1], gi_sem.at[1])
    up[...] = gi[far] + rgi[1]
    send(up, rgi.at[2], gi_sem.at[2], (gz, far))
    for side in (0, 2):
        arrived(xc.at[core, side], xc_sem.at[core, side])
        arrived(xc.at[diag, side], xc_sem.at[diag, side])

    for a in range(3):
        plane = xc[:, a].reshape(128, YX)
        for e in range(3):
            line = shifted(plane, 0, e - 1)
            for b in range(3):
                tap = 9 * a + 3 * b + e
                xp[tap * 128:(tap + 1) * 128, :] = shifted(line, b - 1, 0)
    y_ref[0] = jnp.dot(wy_ref[...], xp[...], preferred_element_type=F32).astype(BF)

    for zj in ring:
        arrived(rp.at[zj], rp_sem.at[zj])
        arrived(sp.at[2 + zj], sp_sem.at[2 + zj])
    for owner, slot, source in forwards:
        @pl.when(z != owner)
        def _():
            arrived(sp.at[slot], sp_sem.at[slot])

    da[...] = jnp.zeros((784, 128), F32)
    db[...] = jnp.zeros((784, 128), F32)
    edge_plane = jnp.where(k < 4, 0, 7)

    def variants(value, unit, at, size):
        out = []
        for delta in (-2, -1, 0, 1, 2):
            inside = jnp.logical_and(at - delta >= 0, at - delta < size)
            out.append(value if delta == 0 else moved(value, -delta * unit) * keep(inside))
        out.append(value * keep(at >= 1))
        out.append(value * keep(at < size - 1))
        return out

    @pl.loop(0, 8)
    def _(v):
        rows = rp[v]
        for tx, line in enumerate(variants(rows, 1, place, SIDE)):
            for ty, plane in enumerate(variants(line, SIDE, row, SIDE)):
                at = (ty * 7 + tx) * 16
                rv[at:at + 16, :] = plane
        near = sp[pl.ds(v, 5)].reshape(160, YX)
        flag = jnp.where(v == edge_plane, 1.0, 0.0).astype(BF)
        columns = jnp.concatenate([near, sp[v + 2] * flag], axis=0)
        part = lax.dot_general(rv[...], columns, NT, preferred_element_type=F32)
        da[...] += part[:, 0:128]
        db[:, 0:64] += part[:, 128:192]

    lane = lax.broadcasted_iota(jnp.int32, (49, 128), 1)
    for kj in range(8):
        tails = []
        for p in range(2):
            mp[kj, p] = da[pl.ds(2 * kj + p, 49, stride=16), :]
            tails.append(db[pl.ds(2 * kj + p, 49, stride=16), :])
        mp[kj, 2] = jnp.where(lane < 64, tails[0], pltpu.roll(tails[1], shift=64, axis=1))
    for kj in peers:
        send(mp.at[kj], rpf.at[k], rpf_sem.at[k], (kj * 8 + z, col))

    total = mg[k]
    for kj in peers:
        arrived(rg.at[kj], rg_sem.at[kj])
        total = total + rg[kj]
    for j in range(14):
        for zj in range(8):
            b3[zj, 2 * j:2 * j + 2, :] = total[2 * zj:2 * zj + 2, 128 * j:128 * j + 128]
    halves = (total[:, 1792:1920], pltpu.roll(total[:, 1792:1920], shift=64, axis=1))
    for zj in range(8):
        b3[zj, 28:32, :] = halves[zj // 4][4 * (zj % 4):4 * (zj % 4) + 4]
    for zj in ring:
        send(b3.at[zj], rb.at[z], rb_sem.at[z], (k * 8 + zj, col))

    arrived(rgi.at[0], gi_sem.at[0])
    arrived(rgi.at[2], gi_sem.at[2])
    gi_ref[0] = (gi[col] + rgi[0] + rgi[2]).astype(BF)

    for kj in peers:
        arrived(rpf.at[kj], rpf_sem.at[kj])
    rpf[k] = mp[k]
    heads = [rpf[0, p] for p in range(2)]
    tail = rpf[0, 2]
    low, high = rpf[0, 2], rpf[7, 2]
    for kj in range(1, 8):
        heads = [heads[p] + rpf[kj, p] for p in range(2)]
        tail = tail + rpf[kj, 2]
    pad = jnp.zeros((49, 32), F32)
    for p in range(2):
        m2, m1, zero, p1 = [heads[p][:, 32 * i:32 * i + 32] for i in range(4)]
        p2 = tail[:, 64 * p:64 * p + 32]
        first = low[:, 64 * p + 32:64 * p + 64]
        last = high[:, 64 * p + 32:64 * p + 64]
        wide = jnp.concatenate(
            [zero - last, p1, p2, pad, m1, zero, p1, pad, m2, m1, zero - first, pad], axis=1)
        for part in range(3):
            piece = wide.astype(BF)
            wide = wide - piece.astype(F32)
            picked = jnp.dot(choice_ref[...], piece, preferred_element_type=F32).astype(BF)
            for a in range(3):
                at = (part * 6 + p * 3 + a) * 16
                for be in range(9):
                    lh[at:at + 16, be * 128:be * 128 + 128] = picked[be * 16:be * 16 + 16, a * 128:a * 128 + 128]
    factor = jnp.dot(lh[...], column_ref[...], preferred_element_type=F32)
    factor = (factor[0:96] + factor[96:192] + factor[192:288]) * (1.0 / 65536)
    for block in range(6):
        pf_ref[block * 9:block * 9 + 9, :] = factor[block * 16:block * 16 + 9]

    total = b3[z]
    for zj in ring:
        arrived(rb.at[zj], rb_sem.at[zj])
        total = total + rb[zj]
    gf_ref[...] = total[28:32, 0:64] * (1.0 / 65536)
    for tap in range(TAPS):
        for p in range(2):
            at = 2 * (tap // 2) + p
            gw_ref[p * 27 + tap:p * 27 + tap + 1, :] = total[at:at + 1, 64 * (tap % 2):64 * (tap % 2) + 64] * (1.0 / 256)

    for copy in sends:
        copy.wait_send()

    @pl.when(has_skip)
    def _():
        skip_copy().wait_send()

    for owner, slot, source in forwards:
        @pl.when(z == owner)
        def _():
            for copy in forward_copies(owner, slot, source):
                copy.wait_send()


def shards(x_field, weights, grad_out):
    taps = weights.reshape(64, 128, TAPS)
    wy = jnp.transpose(taps, (0, 2, 1)).reshape(64, TAPS * 128)
    wg = jnp.transpose(taps, (1, 2, 0)).reshape(128, TAPS * 64)
    vmem = pl.BlockSpec(memory_space=pltpu.VMEM)
    dma = pltpu.SemaphoreType.DMA
    return pl.pallas_call(
        kernel,
        out_shape=(
            jax.ShapeDtypeStruct((1, 64, YX), BF),
            jax.ShapeDtypeStruct((1, 32, YX), BF),
            jax.ShapeDtypeStruct((54, 64), F32),
            jax.ShapeDtypeStruct((54, 864), F32),
            jax.ShapeDtypeStruct((4, 64), F32),
        ),
        in_specs=[vmem] * 7,
        out_specs=(vmem,) * 5,
        scratch_shapes=[
            pltpu.VMEM((4, 3, 32, YX), BF),
            pltpu.VMEM((4, 64, YX), BF),
            pltpu.VMEM((2, 64, YX), BF),
            pltpu.VMEM((12, 32, YX), BF),
            pltpu.VMEM((8, 16, YX), BF),
            pltpu.VMEM((8, 16, YX), BF),
            pltpu.VMEM((3456, YX), BF),
            pltpu.VMEM((1728, YX), BF),
            pltpu.VMEM((784, YX), BF),
            pltpu.VMEM((784, 128), F32),
            pltpu.VMEM((784, 128), F32),
            pltpu.VMEM((8, 16, 1920), F32),
            pltpu.VMEM((8, 16, 1920), F32),
            pltpu.VMEM((8, 32, 128), F32),
            pltpu.VMEM((8, 32, 128), F32),
            pltpu.VMEM((8, 3, 49, 128), F32),
            pltpu.VMEM((8, 3, 49, 128), F32),
            pltpu.VMEM((4, 32, YX), F32),
            pltpu.VMEM((3, 32, YX), F32),
            pltpu.VMEM((32, YX), F32),
            pltpu.VMEM((288, 1152), BF),
            dma((64,)),
            dma((8,)),
            dma((4, 3)),
            dma((4,)),
            dma((2,)),
            dma((12,)),
            dma((8,)),
            dma((8,)),
            dma((8,)),
            dma((8,)),
            dma((3,)),
        ],
        compiler_params=pltpu.CompilerParams(
            collective_id=0, has_side_effects=True, vmem_limit_bytes=48 * 2**20),
    )(x_field.reshape(32, YX), grad_out.reshape(64, YX), wy, wg,
      jnp.asarray(channel_order(), BF), jnp.asarray(type_choice(), BF), jnp.asarray(column_order(), BF))


def solution(mesh):
    return jax.shard_map(
        shards,
        mesh=mesh,
        in_specs=(P("gz", "col", None), P("col", None), P("gz", "col", None)),
        out_specs=(
            P("gz", "col", None),
            P("gz", "col", None),
            P("gz", "col"),
            P("gz", "col"),
            P("gz", "col"),
        ),
        check_vma=False,
    )
```

time: 713 us -> 71.9 us (0.10)
  blocking collectives: 317 us -> 0 us
  waiting for transfers between devices: 126 us -> 0 us
  local copies, waits for them, and re-layouts: 134 us -> 11.8 us
  starting transfers between devices: 86.6 us -> 0 us
  Pallas kernels: 0 us -> 58.3 us
  matrix products: 27.8 us -> 0 us
  between operations: 16.9 us -> 0.76 us
    unnamed x2 -> x0, blocking collectives: 297 us -> none
    unnamed x22 -> x0, waiting for transfers between devices: 126 us -> none
    another operation x3 -> x0, local copies, waits for them, and re-layouts: 76.6 us -> none  [the longest x2 38.3 us: patch_columns(): stacked = jnp.stack(pieces, axis=2)]
    unnamed x21 -> x0, starting transfers between devices: 75.5 us -> none
    pallas_call x0 -> x1, Pallas kernels: none -> 58.3 us  [shards(): pl.pallas_call(kernel, out_shape=(jax.ShapeDtypeStruct((1, 64, YX), BF),...]
    unnamed x62 -> x19, local copies, waits for them, and re-layouts: 37.8 us -> 5.76 us
    dot_general x31 -> x0, matrix products: 27.8 us -> none  [the longest x3 17 us: contract_cells(): lax.dot_general(left, right, (((1,), (1,)), ((), ())), preferred_element_...]
    all_gather x2 -> x0, blocking collectives: 19.9 us -> none  [the longest x1 10.2 us: shards(): x_all = lax.all_gather(x_ext, 'col', axis=1, tiled=True)]
  transfers between devices with their start and end apart: 25 -> 0, of which waited for: 2 -> 0; matrix products, arithmetic and copies ran while one was open for 48% -> 0% of each run, Pallas kernels for 0% -> 0%
where the time goes in v1:
time: 71.9 us; the launch traced here: 70.8 us
  Pallas kernels  58.3 us (81%)
  local copies, waits for them, and re-layouts  11.8 us (16%)
  between operations  0.76 us (1%)
    pallas_call x1, Pallas kernels, shards(): pl.pallas_call(kernel, out_shape=(jax.ShapeDtypeStruct((1, 64, YX), BF),...  58.3 us
    unnamed x19, local copies, waits for them, and re-layouts  5.76 us
    transpose x1, local copies, waits for them, and re-layouts, shards(): wg = jnp.transpose(taps, (1, 2, 0)).reshape(128, TAPS * 64)  3 us
    transpose x1, local copies, waits for them, and re-layouts, shards(): wy = jnp.transpose(taps, (0, 2, 1)).reshape(64, TAPS * 128)  1.54 us

profile of v1, /device:TPU:1, one launch (start us, length us, event | category | flops | bytes accessed | tf_op | source)
XLA Modules:
  0.0 70.8 jit_solution(3330484567338998407)
XLA Ops:
  0.6 1.4 %copy.13 = bf16[64,3456]{0,1:T(8,128)(2,1)S(1)} copy(bf16[64,3456]{1,0:T(8,128)(2,1)} %param.7) | data formatting | bytes 884736 | tf_op args[1]
  2.1 0.2 reshape.27
  2.3 0.0 copy-start.5
  2.3 1.0 %copy-done.5 = bf16[64,128,27]{0,2,1:T(8,128)(2,1)} copy-done((bf16[64,128,27]{0,2,1:T(8,128)(2,1)}, bf16[64,128,27]{0,2,1:T(8,128)(2,1)S(1)}, u32[]{:S(2)}) %copy-start.5) | copy-done | bytes 442392
  3.3 1.5 %copy.14 = bf16[64,27,128]{2,1,0:T(8,128)(2,1)S(1)} copy(bf16[64,27,128]{0,1,2:T(8,128)(2,1)S(1)} %bitcast.14) | data formatting | bytes 884736 | tf_op jit(solution)/shard_map/transpose | solution.py:368
  4.8 0.0 copy-start
  4.9 0.0 copy-start.1
  4.9 0.0 copy-start.2
  4.9 0.0 copy-start.3
  4.9 0.0 copy-start.4
  4.9 0.2 copy.19
  5.1 3.0 %copy.15 = bf16[128,27,64]{0,2,1:T(8,128)(2,1)} copy(bf16[128,27,64]{2,1,0:T(8,128)(2,1)} %bitcast.15) | data formatting | bytes 884736 | tf_op jit(solution)/shard_map/transpose | solution.py:369
  8.1 1.2 %copy.16.wg_ref = bf16[128,1728]{1,0:T(8,128)(2,1)S(1)} copy(bf16[128,1728]{0,1:T(8,128)(2,1)} %bitcast.17) | data formatting | bytes 884736 | tf_op jit(solution)/shard_map/reshape | solution.py:369
  9.3 0.0 copy-done
  9.3 0.0 copy-done.1
  9.3 0.0 copy-done.2
  9.3 0.0 copy-done.3
  9.4 0.0 copy-done.4
  9.4 58.3 %shard_map.101 = (bf16[1,64,1024]{2,1,0:T(8,128)(2,1)S(1)}, bf16[1,32,1024]{2,1,0:T(8,128)(2,1)S(1)}, f32[54,64]{1,0:T(8,128)S(1)}, f32[54,864]{1,0:T(8,128)S(1)}, f32[4,64]{1,0:T(4,128)S(1)}) custom-call(bf16[32,1024]{1,0:T(8,128)(2,1)S(1)} %bitcast.13, bf16[64,1024]{1,0:T(8,128)(2,1)S(1)} %bitcast.12, bf16[64,3456]{1,0:T(8,128)(2,1)S(1)} %bitcast.11, ...), custom_call_target="tpu_custom_call" | custom-call | tf_op jit(solution)/shard_map/pallas_call | solution.py:372
  67.6 0.7 copy.25
  68.3 0.6 copy.26
  68.9 0.6 copy.27
  69.5 0.7 copy.28
  70.2 0.6 copy.29
Async XLA Ops:
  2.3 1.0 %copy-start.5 = (bf16[64,128,27]{0,2,1:T(8,128)(2,1)}, bf16[64,128,27]{0,2,1:T(8,128)(2,1)S(1)}, u32[]{:S(2)}) copy-start(bf16[64,128,27]{0,2,1:T(8,128)(2,1)S(1)} %reshape.27) | copy-start | bytes 1327108
  4.8 4.5 %copy-start = (bf16[1152,864]{1,0:T(8,128)(2,1)S(1)}, bf16[1152,864]{1,0:T(8,128)(2,1)}, u32[]{:S(2)}) copy-start(bf16[1152,864]{1,0:T(8,128)(2,1)} %constant.8.clone.column_ref) | copy-start | bytes 5971972
  4.9 4.5 %copy-start.1 = (bf16[1,64,1024]{2,1,0:T(8,128)(2,1)S(1)}, bf16[1,64,1024]{2,1,0:T(8,128)(2,1)}, u32[]{:S(2)}) copy-start(bf16[1,64,1024]{2,1,0:T(8,128)(2,1)} %param.8) | copy-start | bytes 393220
  4.9 4.5 %copy-start.2 = (bf16[1,32,1024]{2,1,0:T(8,128)(2,1)S(1)}, bf16[1,32,1024]{2,1,0:T(8,128)(2,1)}, u32[]{:S(2)}) copy-start(bf16[1,32,1024]{2,1,0:T(8,128)(2,1)} %param.6) | copy-start | bytes 196612
  4.9 4.5 %copy-start.3 = (bf16[144,49]{1,0:T(8,128)(2,1)S(1)}, bf16[144,49]{1,0:T(8,128)(2,1)}, u32[]{:S(2)}) copy-start(bf16[144,49]{1,0:T(8,128)(2,1)} %constant.7.clone.choice_ref) | copy-start | bytes 42340
  4.9 4.5 %copy-start.4 = (bf16[128,128]{1,0:T(8,128)(2,1)S(1)}, bf16[128,128]{1,0:T(8,128)(2,1)}, u32[]{:S(2)}) copy-start(bf16[128,128]{1,0:T(8,128)(2,1)} %constant.6.clone.order_ref) | copy-start | bytes 98308

commit v2 on v1

v2 whole, which is shorter than its diff:
```python
import jax
import jax.numpy as jnp
import numpy as np
from jax import lax
from jax.experimental import pallas as pl
from jax.experimental.pallas import tpu as pltpu
from jax.sharding import PartitionSpec as P

MESH = pl.DeviceIdType.MESH
BF, F32 = jnp.bfloat16, jnp.float32
SIDE, YX, TAPS = 32, 1024, 27
NT = (((1,), (1,)), ((), ()))


def kind(first, second):
    if first != second:
        return second - first + 2
    return {1: 2, 2: 5, 0: 6}[first]


def channel_order():
    out = np.zeros((128, 128), np.float32)
    for v in range(8):
        for k in range(8):
            for p in range(2):
                out[v * 16 + 2 * k + p, k // 2 * 32 + v * 4 + 2 * (k % 2) + p] = 1
    return out


def type_choice():
    out = np.zeros((144, 49), np.float32)
    for b2 in range(3):
        for e2 in range(3):
            for b in range(3):
                for e in range(3):
                    out[(b2 * 3 + e2) * 16 + b * 3 + e, kind(b, b2) * 7 + kind(e, e2)] = 1
    return out


def moved(value, step):
    step = step % YX
    return value if step == 0 else pltpu.roll(value, shift=(YX - step) % YX, axis=1)


def cell_masks():
    cell = lax.broadcasted_iota(jnp.int32, (1, YX), 1)
    return cell // SIDE, cell % SIDE


def keep(where):
    return where.astype(F32).astype(BF)


def kernel(x_hbm, g_hbm, w_hbm, order_hbm, choice_hbm,
           y_ref, gi_ref, gw_ref, pf_ref, gf_ref,
           g_ref, w_ref, order_ref, choice_ref, column_ref, wt, wy, wg,
           xc, gc, gs, sp, r4, rp, r9, xp, gp, rv, da, db, ga, gb, mg, rg, b3, rb, mp, rpf, mw, rw, me, re, gi, rgi, up, lh,
           send_sem, late_sem, load_sem, xc_sem, gc_sem, gs_sem, sp_sem, r4_sem, rg_sem, rb_sem, rpf_sem, rw_sem, re_sem,
           gi_sem):
    gz, col = lax.axis_index("gz"), lax.axis_index("col")
    k, z = gz // 8, gz % 8
    core = col + 1 - 2 * (col % 2)
    far = (col + 2) % 4
    diag = (core + 2) % 4
    ring = [(z + j) % 8 for j in (1, 7, 2, 6, 3, 5, 4)]
    peers = [(k + j) % 8 for j in range(1, 8)]
    x_own, g_own = x_hbm.at[0], g_hbm.at[0]

    def on_ring(offset):
        return (k * 8 + (z + offset) % 8, col)

    sends = []

    def send(src, dst, sem, target):
        copy = pltpu.make_async_remote_copy(
            src_ref=src, dst_ref=dst, send_sem=send_sem.at[len(sends)], recv_sem=sem,
            device_id=target, device_id_type=MESH)
        copy.start()
        sends.append(copy)

    def arrived(dst, sem):
        pltpu.make_async_remote_copy(
            src_ref=dst, dst_ref=dst, send_sem=send_sem.at[0], recv_sem=sem,
            device_id=(gz, core), device_id_type=MESH).wait_recv()

    loads = [pltpu.make_async_copy(src, dst, load_sem.at[i]) for i, (src, dst) in enumerate((
        (w_hbm, w_ref), (g_own, g_ref), (x_own, xc.at[col, 1]), (x_own, sp.at[2 + z]), (g_own, gc.at[col]), (g_own, gs.at[1 + z]),
        (order_hbm, order_ref), (choice_hbm, choice_ref)))]
    for load in loads:
        load.start()

    barrier = pltpu.get_barrier_semaphore()
    partners = [(gz, core), (gz, far)]
    partners += [(k * 8 + zj, col) for zj in ring] + [(kj * 8 + z, col) for kj in peers]
    for target in partners:
        pl.semaphore_signal(barrier, inc=1, device_id=target, device_id_type=MESH)
    loads[0].wait()
    wt[:, 0:64] = jnp.transpose(w_ref[...].astype(F32))
    wt[:, 64:128] = jnp.zeros((3456, 64), F32)
    for tap in range(TAPS):
        block = wt[pl.ds(tap, 128, stride=TAPS), :]
        wg[:, tap * 64:tap * 64 + 64] = block[:, 0:64].astype(BF)
        wy[:, tap * 128:tap * 128 + 128] = jnp.transpose(block)[0:64].astype(BF)
    entry = lax.broadcasted_iota(jnp.int32, (128, 864), 0)
    column = lax.broadcasted_iota(jnp.int32, (128, 864), 1)
    home = jnp.where(entry < 96, entry % 32 * 27 + entry // 32 * 9, -27)
    for be in range(9):
        column_ref[be * 128:be * 128 + 128, :] = keep(column == home + be)
    for load in loads[1:]:
        load.wait()

    row, place = cell_masks()
    in_row = {-1: keep(place >= 1), 1: keep(place < SIDE - 1)}
    in_plane = {-1: keep(row >= 1), 1: keep(row < SIDE - 1)}

    def shifted(value, dy, dx):
        if dx:
            value = moved(value, dx) * in_row[dx]
        if dy:
            value = moved(value, SIDE * dy) * in_plane[dy]
        return value

    def cotangent_taps(a, plane):
        for e in range(3):
            line = shifted(plane, 0, 1 - e)
            for b in range(3):
                tap = 9 * a + 3 * b + e
                gp[tap * 64:(tap + 1) * 64, :] = shifted(line, 1 - b, 0)

    cotangent_taps(1, g_ref[...])
    pl.semaphore_wait(barrier, len(partners))

    def edge_copies(buf, sem, base, edges):
        return [(plane, pltpu.make_async_remote_copy(
            src_ref=buf.at[base + plane], dst_ref=buf.at[home], send_sem=late_sem.at[late], recv_sem=sem.at[home],
            device_id=((k + step) % 8 * 8 + z, col), device_id_type=MESH)) for plane, home, step, late in edges]

    x_edges = edge_copies(sp, sp_sem, 2, ((0, 10, 7, 0), (1, 11, 7, 1), (6, 0, 1, 2), (7, 1, 1, 3)))
    g_edges = edge_copies(gs, gs_sem, 1, ((0, 9, 7, 4), (7, 0, 1, 5)))

    def pass_on(buf, sem, base, edges, offset, steps):
        at = (z + offset) % 8
        slot = base + at
        if offset:
            arrived(buf.at[slot], sem.at[slot])
        for step in steps:
            send(buf.at[slot], buf.at[slot], sem.at[slot], on_ring(step))
        for plane, copy in edges:
            @pl.when(at == plane)
            def _():
                copy.start()

    def pass_x(offset, *steps):
        pass_on(sp, sp_sem, 2, x_edges, offset, steps)

    def pass_g(offset, *steps):
        pass_on(gs, gs_sem, 1, g_edges, offset, steps)

    def others(buf, sem):
        send(buf, buf, sem, (gz, far))
        send(buf, buf, sem, (gz, core))

    def hand_over(buf, sem):
        arrived(buf, sem)
        send(buf, buf, sem, (gz, core))

    pass_x(0, 1, 7)
    others(xc.at[col, 1], xc_sem.at[col, 1])
    pass_g(0, 1, 7)
    pass_x(7, 1)
    pass_x(1, 7)
    hand_over(xc.at[far, 1], xc_sem.at[far, 1])
    pass_x(6, 1)
    pass_x(2, 7)
    pass_g(7, 1)
    pass_g(1, 7)
    pass_x(5, 1)
    pass_x(3)
    pass_x(4)

    pick = lax.broadcasted_iota(jnp.int32, (32, 256), 0)
    source = lax.broadcasted_iota(jnp.int32, (32, 256), 1)
    wanted = pick // 4 * 32 + pick // 2 % 2 * 16 + 2 * z + pick % 2
    r4[col] = jnp.dot(keep(source == wanted), sp[2:10].reshape(256, YX), preferred_element_type=F32).astype(BF)
    others(r4.at[col], r4_sem.at[col])
    others(gc.at[col], gc_sem.at[col])
    pass_g(6, 1)
    pass_g(2, 7)
    hand_over(r4.at[far], r4_sem.at[far])
    arrived(r4.at[core], r4_sem.at[core])
    arrived(r4.at[diag], r4_sem.at[diag])
    rp[...] = jnp.dot(
        order_ref[...], r4[...].reshape(128, YX), preferred_element_type=F32).astype(BF).reshape(8, 16, YX)

    da[...] = jnp.zeros((784, 128), F32)
    db[...] = jnp.zeros((800, 128), F32)
    edge_plane = jnp.where(k < 4, 0, 7)

    def variants(value, unit, at, size):
        out = []
        for delta in (-2, -1, 0, 1, 2):
            inside = jnp.logical_and(at - delta >= 0, at - delta < size)
            out.append(value if delta == 0 else moved(value, -delta * unit) * keep(inside))
        out.append(value * keep(at >= 1))
        out.append(value * keep(at < size - 1))
        return out

    def factor_plane(v):
        rows = rp[v]
        for tx, line in enumerate(variants(rows, 1, place, SIDE)):
            for ty, plane in enumerate(variants(line, SIDE, row, SIDE)):
                at = (ty * 7 + tx) * 16
                rv[at:at + 16, :] = plane
        for b in range(3):
            for e in range(3):
                at = ((3 - b) * 7 + 3 - e) * 16
                r9[v, (3 * b + e) * 16:(3 * b + e) * 16 + 16, :] = rv[at:at + 16, :]
        beside = sp[pl.ds(v, 5)].reshape(160, YX)
        flag = jnp.where(v == edge_plane, 1.0, 0.0).astype(BF)
        columns = jnp.concatenate([beside, sp[v + 2] * flag], axis=0)
        part = lax.dot_general(rv[...], columns, NT, preferred_element_type=F32)
        da[...] += part[:, 0:128]
        db[0:784, 0:64] += part[:, 128:192]

    @pl.loop(2, 4)
    def _(v):
        factor_plane(v)

    pass_g(5, 1)
    pass_g(3)

    @pl.loop(4, 6)
    def _(v):
        factor_plane(v)

    pass_g(4)
    hand_over(gc.at[far], gc_sem.at[far])
    for buf, sem, slot, edge in ((sp, sp_sem, 0, 0), (sp, sp_sem, 1, 0), (sp, sp_sem, 10, 7), (sp, sp_sem, 11, 7)):
        arrived(buf.at[slot], sem.at[slot])

        @pl.when(k == edge)
        def _():
            buf[slot] = jnp.zeros(buf.shape[1:], BF)

    for side in (0, 2):
        xc[col, side] = sp[1 + z + side]
        others(xc.at[col, side], xc_sem.at[col, side])

    @pl.loop(6, 10)
    def _(v):
        factor_plane(v % 8)

    lane = lax.broadcasted_iota(jnp.int32, (25, 128), 1)

    def packed(kj, first):
        out = None
        for q in range(4):
            run = db[pl.ds(2 * kj + q // 2 + 400 * (q % 2), 25, stride=16), :]
            step = (32 * q - first) % 128
            run = pltpu.roll(run, shift=step, axis=1) if step else run
            out = run if out is None else jnp.where(lane // 32 == q, run, out)
        return out

    for kj in range(8):
        for p in range(2):
            mp[kj, 49 * p:49 * p + 49] = da[pl.ds(2 * kj + p, 49, stride=16), :]
        mp[kj, 98:123] = packed(kj, 0)
    for kj in peers:
        send(mp.at[kj], rpf.at[k], rpf_sem.at[k], (kj * 8 + z, col))
    def face_copies(owner):
        return [pltpu.make_async_remote_copy(
            src_ref=me.at[(owner + j) % 8], dst_ref=re.at[owner // 7], send_sem=late_sem.at[24 + j],
            recv_sem=re_sem.at[owner // 7], device_id=((owner + j) % 8 * 8 + z, col),
            device_id_type=MESH) for j in range(1, 8)]

    for owner in (0, 7):
        @pl.when(k == owner)
        def _():
            for kj in range(8):
                me[kj] = packed(kj, 32)
            for copy in face_copies(owner):
                copy.start()
            re[owner // 7] = me[owner]

    for slot, edge in ((0, 0), (9, 7)):
        arrived(gs.at[slot], gs_sem.at[slot])

        @pl.when(k == edge)
        def _():
            gs[slot] = jnp.zeros((64, YX), BF)

    cotangent_taps(0, gs[2 + z])
    cotangent_taps(2, gs[z])
    gi[...] = jnp.dot(wg[...], gp[...], preferred_element_type=F32).reshape(4, 32, YX)
    send(gi.at[core], rgi.at[0], gi_sem.at[0], (gz, core))
    send(gi.at[diag], rgi.at[1], gi_sem.at[1], (gz, core))

    ga[...] = jnp.zeros((144, 128), F32)
    gb[...] = jnp.zeros((144, 128), F32)

    @pl.loop(0, 8)
    def _(v):
        part = lax.dot_general(
            r9[v], gs[pl.ds(v, 3)].reshape(192, YX), NT, preferred_element_type=F32)
        ga[...] += part[:, 0:128]
        gb[:, 0:64] += part[:, 128:192]

    wide_lane = lax.broadcasted_iota(jnp.int32, (9, 128), 1)
    for kj in range(8):
        tails = []
        for p in range(2):
            mw[kj, 9 * p:9 * p + 9] = ga[pl.ds(2 * kj + p, 9, stride=16), :]
            tails.append(gb[pl.ds(2 * kj + p, 9, stride=16), :])
        mw[kj, 18:27] = jnp.where(wide_lane < 64, tails[0], pltpu.roll(tails[1], shift=64, axis=1))
    for kj in peers:
        send(mw.at[kj], rw.at[k], rw_sem.at[k], (kj * 8 + z, col))

    arrived(gc.at[core], gc_sem.at[core])
    arrived(gc.at[diag], gc_sem.at[diag])
    gram = lax.dot_general(gc[...].reshape(256, YX), g_ref[...], NT, preferred_element_type=F32)
    for kj in range(8):
        mg[kj, :, 0:64] = gram[32 * kj:32 * kj + 16]
        mg[kj, :, 64:128] = gram[32 * kj + 16:32 * kj + 32]
    for kj in peers:
        send(mg.at[kj], rg.at[k], rg_sem.at[k], (kj * 8 + z, col))

    arrived(rgi.at[1], gi_sem.at[1])
    up[...] = gi[far] + rgi[1]
    send(up, rgi.at[2], gi_sem.at[2], (gz, far))
    for side in (0, 2):
        hand_over(xc.at[far, side], xc_sem.at[far, side])

    arrived(xc.at[core, 1], xc_sem.at[core, 1])
    arrived(xc.at[diag, 1], xc_sem.at[diag, 1])
    for side in (0, 2):
        arrived(xc.at[core, side], xc_sem.at[core, side])
        arrived(xc.at[diag, side], xc_sem.at[diag, side])

    for a in range(3):
        plane = xc[:, a].reshape(128, YX)
        for e in range(3):
            line = shifted(plane, 0, e - 1)
            for b in range(3):
                tap = 9 * a + 3 * b + e
                xp[tap * 128:(tap + 1) * 128, :] = shifted(line, b - 1, 0)
    y_ref[0] = jnp.dot(wy[...], xp[...], preferred_element_type=F32).astype(BF)

    total = mg[k]
    for kj in peers:
        arrived(rg.at[kj], rg_sem.at[kj])
        total = total + rg[kj]
    halves = (total, pltpu.roll(total, shift=64, axis=1))
    for zj in range(8):
        b3[zj] = halves[zj // 4][4 * (zj % 4):4 * (zj % 4) + 4]
    for zj in ring:
        send(b3.at[zj], rb.at[z], rb_sem.at[z], (k * 8 + zj, col))

    arrived(rgi.at[0], gi_sem.at[0])
    arrived(rgi.at[2], gi_sem.at[2])
    gi_ref[0] = (gi[col] + rgi[0] + rgi[2]).astype(BF)

    total = mp[k]
    for kj in peers:
        arrived(rpf.at[kj], rpf_sem.at[kj])
        total = total + rpf[kj]
    for owner in (0, 7):
        @pl.when(k != owner)
        def _():
            arrived(re.at[owner // 7], re_sem.at[owner // 7])
    low, high = re[0], re[1]
    pad = jnp.zeros((49, 32), F32)

    def unpacked(value, p):
        at = 64 * p
        return jnp.concatenate([value[0:25, at:at + 32], value[0:24, at + 32:at + 64]], axis=0)

    for p in range(2):
        head = total[49 * p:49 * p + 49]
        m2, m1, zero, p1 = [head[:, 32 * i:32 * i + 32] for i in range(4)]
        p2 = unpacked(total[98:123], p)
        first, last = unpacked(low, p), unpacked(high, p)
        wide = jnp.concatenate(
            [zero - last, p1, p2, pad, m1, zero, p1, pad, m2, m1, zero - first, pad], axis=1)
        for part in range(3):
            piece = wide.astype(BF)
            wide = wide - piece.astype(F32)
            picked = jnp.dot(choice_ref[...], piece, preferred_element_type=F32).astype(BF)
            for a in range(3):
                at = (part * 6 + p * 3 + a) * 16
                for be in range(9):
                    lh[at:at + 16, be * 128:be * 128 + 128] = picked[be * 16:be * 16 + 16, a * 128:a * 128 + 128]
    factor = jnp.dot(lh[...], column_ref[...], preferred_element_type=F32)
    factor = (factor[0:96] + factor[96:192] + factor[192:288]) * (1.0 / 65536)
    for block in range(6):
        pf_ref[block * 9:block * 9 + 9, :] = factor[block * 16:block * 16 + 9]

    total = mw[k]
    for kj in peers:
        arrived(rw.at[kj], rw_sem.at[kj])
        total = total + rw[kj]
    total = total * (1.0 / 256)
    for p in range(2):
        gw_ref[p * 27:p * 27 + 9, :] = total[18:27, 64 * p:64 * p + 64]
        gw_ref[p * 27 + 9:p * 27 + 18, :] = total[9 * p:9 * p + 9, 64:128]
        gw_ref[p * 27 + 18:p * 27 + 27, :] = total[9 * p:9 * p + 9, 0:64]

    total = b3[z]
    for zj in ring:
        arrived(rb.at[zj], rb_sem.at[zj])
        total = total + rb[zj]
    gf_ref[...] = total[:, 0:64] * (1.0 / 65536)

    for _, copy in x_edges + g_edges:
        copy.wait_send()
    for copy in sends:
        copy.wait_send()
    for owner in (0, 7):
        @pl.when(k == owner)
        def _():
            for copy in face_copies(owner):
                copy.wait_send()


def shards(x_field, weights, grad_out):
    vmem = pl.BlockSpec(memory_space=pltpu.VMEM)
    there = pl.BlockSpec(memory_space=pl.ANY)
    dma = pltpu.SemaphoreType.DMA
    return pl.pallas_call(
        kernel,
        out_shape=(
            jax.ShapeDtypeStruct((1, 64, YX), BF),
            jax.ShapeDtypeStruct((1, 32, YX), BF),
            jax.ShapeDtypeStruct((54, 64), F32),
            jax.ShapeDtypeStruct((54, 864), F32),
            jax.ShapeDtypeStruct((4, 64), F32),
        ),
        in_specs=[there] * 5,
        out_specs=(vmem,) * 5,
        scratch_shapes=[
            pltpu.VMEM((64, YX), BF),
            pltpu.VMEM((64, 3456), BF),
            pltpu.VMEM((128, 128), BF),
            pltpu.VMEM((144, 49), BF),
            pltpu.VMEM((1152, 864), BF),
            pltpu.VMEM((3456, 128), F32),
            pltpu.VMEM((64, 3456), BF),
            pltpu.VMEM((128, 1728), BF),
            pltpu.VMEM((4, 3, 32, YX), BF),
            pltpu.VMEM((4, 64, YX), BF),
            pltpu.VMEM((10, 64, YX), BF),
            pltpu.VMEM((12, 32, YX), BF),
            pltpu.VMEM((4, 32, YX), BF),
            pltpu.VMEM((8, 16, YX), BF),
            pltpu.VMEM((8, 144, YX), BF),
            pltpu.VMEM((3456, YX), BF),
            pltpu.VMEM((1728, YX), BF),
            pltpu.VMEM((784, YX), BF),
            pltpu.VMEM((784, 128), F32),
            pltpu.VMEM((800, 128), F32),
            pltpu.VMEM((144, 128), F32),
            pltpu.VMEM((144, 128), F32),
            pltpu.VMEM((8, 16, 128), F32),
            pltpu.VMEM((8, 16, 128), F32),
            pltpu.VMEM((8, 4, 128), F32),
            pltpu.VMEM((8, 4, 128), F32),
            pltpu.VMEM((8, 123, 128), F32),
            pltpu.VMEM((8, 123, 128), F32),
            pltpu.VMEM((8, 27, 128), F32),
            pltpu.VMEM((8, 27, 128), F32),
            pltpu.VMEM((8, 25, 128), F32),
            pltpu.VMEM((2, 25, 128), F32),
            pltpu.VMEM((4, 32, YX), F32),
            pltpu.VMEM((3, 32, YX), F32),
            pltpu.VMEM((32, YX), F32),
            pltpu.VMEM((288, 1152), BF),
            dma((72,)),
            dma((32,)),
            dma((8,)),
            dma((4, 3)),
            dma((4,)),
            dma((10,)),
            dma((12,)),
            dma((4,)),
            dma((8,)),
            dma((8,)),
            dma((8,)),
            dma((8,)),
            dma((2,)),
            dma((3,)),
        ],
        compiler_params=pltpu.CompilerParams(
            collective_id=0, has_side_effects=True, vmem_limit_bytes=56 * 2**20),
    )(x_field, grad_out, weights,
      jnp.asarray(channel_order(), BF), jnp.asarray(type_choice(), BF))


def solution(mesh):
    return jax.shard_map(
        shards,
        mesh=mesh,
        in_specs=(P("gz", "col", None), P("col", None), P("gz", "col", None)),
        out_specs=(
            P("gz", "col", None),
            P("gz", "col", None),
            P("gz", "col"),
            P("gz", "col"),
            P("gz", "col"),
        ),
        check_vma=False,
    )
```

time: 71.9 us -> 64.8 us (0.901); the launches traced: 70.8 us -> 64.6 us
  local copies, waits for them, and re-layouts: 11.8 us -> 4.23 us
  Pallas kernels: 58.3 us -> 59.7 us
    transpose x2 -> x0, local copies, waits for them, and re-layouts: 4.54 us -> none  [the longest x1 3 us: shards(): wg = jnp.transpose(taps, (1, 2, 0)).reshape(128, TAPS * 64)]
    unnamed x19 -> x13, local copies, waits for them, and re-layouts: 5.76 us -> 4.23 us
    reshape x2 -> x0, local copies, waits for them, and re-layouts: 1.46 us -> none  [the longest x1 1.21 us: shards(): wg = jnp.transpose(taps, (1, 2, 0)).reshape(128, TAPS * 64)]
    pallas_call x1, Pallas kernels: 58.3 us -> 59.7 us  [shards(): pl.pallas_call(kernel, out_shape=(jax.ShapeDtypeStruct((1, 64, YX), BF),...]
where the time goes in v2:
time: 64.8 us; the launch traced here: 64.6 us
  Pallas kernels  59.7 us (92%)
  local copies, waits for them, and re-layouts  4.23 us (7%)
  between operations  0.66 us (1%)
    pallas_call x1, Pallas kernels, shards(): pl.pallas_call(kernel, out_shape=(jax.ShapeDtypeStruct((1, 64, YX), BF),...  59.7 us
    unnamed x13, local copies, waits for them, and re-layouts  4.23 us

profile of v2, /device:TPU:1, one launch (start us, length us, event | category | flops | bytes accessed | tf_op | source)
XLA Modules:
  0.0 64.6 jit_solution(11894528705780240478)
XLA Ops:
  0.6 59.7 %shard_map.92 = (bf16[1,64,1024]{2,1,0:T(8,128)(2,1)}, bf16[1,32,1024]{2,1,0:T(8,128)(2,1)}, f32[54,64]{1,0:T(8,128)}, f32[54,864]{1,0:T(8,128)}, f32[4,64]{1,0:T(4,128)}) custom-call(bf16[1,32,1024]{2,1,0:T(8,128)(2,1)} %x_hbm.1, bf16[1,64,1024]{2,1,0:T(8,128)(2,1)} %g_hbm.1, bf16[64,3456]{1,0:T(8,128)(2,1)} %w_hbm.1, ...), custom_call_target="tpu_custom_call" | custom-call | tf_op jit(solution)/shard_map/pallas_call | solution.py:428
  60.3 0.0 copy-start.1
  60.3 0.0 copy-start
  60.3 1.6 %copy.15 = bf16[1,64,1024]{2,1,0:T(8,128)(2,1)} copy(bf16[1,64,1024]{2,1,0:T(8,128)(2,1)} %get-tuple-element.10) | data formatting | bytes 262144
  61.9 0.0 copy-done.1
  61.9 0.0 copy-start.2
  61.9 0.6 copy.16
  62.6 0.1 copy-done.2
  62.7 0.6 copy.17
  63.3 0.0 copy-done
  63.3 0.0 copy-start.3
  63.3 0.7 %copy.18 = f32[54,864]{1,0:T(8,128)} copy(f32[54,864]{1,0:T(8,128)S(1)} %copy-done) | data formatting | bytes 373248
  64.0 0.0 copy-done.3
  64.0 0.6 copy.19
Async XLA Ops:
  60.3 1.6 %copy-start.1 = (bf16[1,32,1024]{2,1,0:T(8,128)(2,1)S(1)}, bf16[1,32,1024]{2,1,0:T(8,128)(2,1)}, u32[]{:S(2)}) copy-start(bf16[1,32,1024]{2,1,0:T(8,128)(2,1)} %get-tuple-element.11) | copy-start | bytes 196612
  60.3 3.0 %copy-start = (f32[54,864]{1,0:T(8,128)S(1)}, f32[54,864]{1,0:T(8,128)}, u32[]{:S(2)}) copy-start(f32[54,864]{1,0:T(8,128)} %get-tuple-element.13) | copy-start | bytes 559876
  61.9 0.7 %copy-start.2 = (f32[54,64]{1,0:T(8,128)S(1)}, f32[54,64]{1,0:T(8,128)}, u32[]{:S(2)}) copy-start(f32[54,64]{1,0:T(8,128)} %get-tuple-element.12) | copy-start | bytes 41476
  63.3 0.7 %copy-start.3 = (f32[4,64]{1,0:T(4,128)S(1)}, f32[4,64]{1,0:T(4,128)}, u32[]{:S(2)}) copy-start(f32[4,64]{1,0:T(4,128)} %get-tuple-element.14) | copy-start | bytes 3076

commit v3 on v2

--- a/solution.py
+++ b/solution.py
@@ -54,8 +54,8 @@
 def kernel(x_hbm, g_hbm, w_hbm, order_hbm, choice_hbm,
            y_ref, gi_ref, gw_ref, pf_ref, gf_ref,
            g_ref, w_ref, order_ref, choice_ref, column_ref, wt, wy, wg,
-           xc, gc, gs, sp, r4, rp, r9, xp, gp, rv, da, db, ga, gb, mg, rg, b3, rb, mp, rpf, mw, rw, me, re, gi, rgi, up, lh,
-           send_sem, late_sem, load_sem, xc_sem, gc_sem, gs_sem, sp_sem, r4_sem, rg_sem, rb_sem, rpf_sem, rw_sem, re_sem,
+           xc, gc, gh, sp, r4, rp, xp, gp, rv, da, db, mg, rg, mx, rx, b3, rb, mp, rpf, me, re, gi, rgi, up, lh,
+           send_sem, late_sem, load_sem, xc_sem, gc_sem, gh_sem, sp_sem, r4_sem, rg_sem, rx_sem, rb_sem, rpf_sem, re_sem,
            gi_sem):
     gz, col = lax.axis_index("gz"), lax.axis_index("col")
     k, z = gz // 8, gz % 8
@@ -83,32 +83,18 @@
             src_ref=dst, dst_ref=dst, send_sem=send_sem.at[0], recv_sem=sem,
             device_id=(gz, core), device_id_type=MESH).wait_recv()
 
+    barrier = pltpu.get_barrier_semaphore()
+    above, below = (gz + 1) % 64, (gz + 63) % 64
+    xl, yk = k // 4, k % 4
+    partners = [(gz, core), (gz, far), (above, col), (below, col)]
+    partners += [(k * 8 + zj, col) for zj in ring] + [(kj * 8 + z, col) for kj in peers]
+    for target in partners:
+        pl.semaphore_signal(barrier, inc=1, device_id=target, device_id_type=MESH)
     loads = [pltpu.make_async_copy(src, dst, load_sem.at[i]) for i, (src, dst) in enumerate((
-        (w_hbm, w_ref), (g_own, g_ref), (x_own, xc.at[col, 1]), (x_own, sp.at[2 + z]), (g_own, gc.at[col]), (g_own, gs.at[1 + z]),
+        (w_hbm, w_ref), (g_own, g_ref), (x_own, xc.at[col, 1]), (x_own, sp.at[2 + z]), (g_own, gc.at[col]),
         (order_hbm, order_ref), (choice_hbm, choice_ref)))]
     for load in loads:
         load.start()
-
-    barrier = pltpu.get_barrier_semaphore()
-    partners = [(gz, core), (gz, far)]
-    partners += [(k * 8 + zj, col) for zj in ring] + [(kj * 8 + z, col) for kj in peers]
-    for target in partners:
-        pl.semaphore_signal(barrier, inc=1, device_id=target, device_id_type=MESH)
-    loads[0].wait()
-    wt[:, 0:64] = jnp.transpose(w_ref[...].astype(F32))
-    wt[:, 64:128] = jnp.zeros((3456, 64), F32)
-    for tap in range(TAPS):
-        block = wt[pl.ds(tap, 128, stride=TAPS), :]
-        wg[:, tap * 64:tap * 64 + 64] = block[:, 0:64].astype(BF)
-        wy[:, tap * 128:tap * 128 + 128] = jnp.transpose(block)[0:64].astype(BF)
-    entry = lax.broadcasted_iota(jnp.int32, (128, 864), 0)
-    column = lax.broadcasted_iota(jnp.int32, (128, 864), 1)
-    home = jnp.where(entry < 96, entry % 32 * 27 + entry // 32 * 9, -27)
-    for be in range(9):
-        column_ref[be * 128:be * 128 + 128, :] = keep(column == home + be)
-    for load in loads[1:]:
-        load.wait()
-
     row, place = cell_masks()
     in_row = {-1: keep(place >= 1), 1: keep(place < SIDE - 1)}
     in_plane = {-1: keep(row >= 1), 1: keep(row < SIDE - 1)}
@@ -127,7 +113,9 @@
                 tap = 9 * a + 3 * b + e
                 gp[tap * 64:(tap + 1) * 64, :] = shifted(line, 1 - b, 0)
 
-    cotangent_taps(1, g_ref[...])
+    x_loads, other_loads = loads[2:4], loads[1:2] + loads[4:]
+    for load in x_loads:
+        load.wait()
     pl.semaphore_wait(barrier, len(partners))
 
     def edge_copies(buf, sem, base, edges):
@@ -136,7 +124,6 @@
             device_id=((k + step) % 8 * 8 + z, col), device_id_type=MESH)) for plane, home, step, late in edges]
 
     x_edges = edge_copies(sp, sp_sem, 2, ((0, 10, 7, 0), (1, 11, 7, 1), (6, 0, 1, 2), (7, 1, 1, 3)))
-    g_edges = edge_copies(gs, gs_sem, 1, ((0, 9, 7, 4), (7, 0, 1, 5)))
 
     def pass_on(buf, sem, base, edges, offset, steps):
         at = (z + offset) % 8
@@ -153,9 +140,6 @@
     def pass_x(offset, *steps):
         pass_on(sp, sp_sem, 2, x_edges, offset, steps)
 
-    def pass_g(offset, *steps):
-        pass_on(gs, gs_sem, 1, g_edges, offset, steps)
-
     def others(buf, sem):
         send(buf, buf, sem, (gz, far))
         send(buf, buf, sem, (gz, core))
@@ -164,18 +148,71 @@
         arrived(buf, sem)
         send(buf, buf, sem, (gz, core))
 
+    def halves(buf, sem, base):
+        rows = buf.shape[1] // 2
+        for offset, step, first in ((5, 1, 0), (3, 7, rows)):
+            slot = base + (z + offset) % 8
+            part = buf.at[slot, pl.ds(first, rows)]
+            send(part, part, sem.at[slot], on_ring(step))
+
     pass_x(0, 1, 7)
+    for load in other_loads:
+        load.wait()
+    send(g_ref, gh.at[0], gh_sem.at[0], (above, col))
+    send(g_ref, gh.at[1], gh_sem.at[1], (below, col))
     others(xc.at[col, 1], xc_sem.at[col, 1])
-    pass_g(0, 1, 7)
+    others(gc.at[col], gc_sem.at[col])
+
+    loads[0].wait()
+    wt[:, 0:64] = jnp.transpose(w_ref[...].astype(F32))
+    wt[:, 64:128] = jnp.zeros((3456, 64), F32)
+    for tap in range(TAPS):
+        block = wt[pl.ds(tap, 128, stride=TAPS), :]
+        wg[:, tap * 64:tap * 64 + 64] = block[:, 0:64].astype(BF)
+        wy[:, tap * 128:tap * 128 + 128] = jnp.transpose(block)[0:64].astype(BF)
+
     pass_x(7, 1)
     pass_x(1, 7)
-    hand_over(xc.at[far, 1], xc_sem.at[far, 1])
+
+    entry = lax.broadcasted_iota(jnp.int32, (128, 864), 0)
+    column = lax.broadcasted_iota(jnp.int32, (128, 864), 1)
+    home = jnp.where(entry < 96, entry % 32 * 27 + entry // 32 * 9, -27)
+    for be in range(9):
+        column_ref[be * 128:be * 128 + 128, :] = keep(column == home + be)
+
+    cotangent_taps(1, g_ref[...])
     pass_x(6, 1)
     pass_x(2, 7)
-    pass_g(7, 1)
-    pass_g(1, 7)
-    pass_x(5, 1)
+    hand_over(xc.at[far, 1], xc_sem.at[far, 1])
+    hand_over(gc.at[far], gc_sem.at[far])
+    pass_x(5)
     pass_x(3)
+    halves(sp, sp_sem, 2)
+    for slot, edge in ((0, 0), (1, 63)):
+        arrived(gh.at[slot], gh_sem.at[slot])
+
+        @pl.when(gz == edge)
+        def _():
+            gh[slot] = jnp.zeros((64, YX), BF)
+
+    cotangent_taps(0, gh[1])
+    cotangent_taps(2, gh[0])
+    arrived(xc.at[core, 1], xc_sem.at[core, 1])
+    arrived(xc.at[diag, 1], xc_sem.at[diag, 1])
+    grad_w = lax.dot_general(xc[:, 1].reshape(128, YX), gp[...], NT, preferred_element_type=F32)
+    for kj in range(8):
+        mg[kj % 4, kj // 4, :, 0:1728] = grad_w[16 * kj:16 * kj + 16]
+        mg[kj % 4, kj // 4, :, 1728:1792] = jnp.zeros((16, 64), F32)
+    arrived(gc.at[core], gc_sem.at[core])
+    arrived(gc.at[diag], gc_sem.at[diag])
+    gram = lax.dot_general(gc[...].reshape(256, YX), g_ref[...], NT, preferred_element_type=F32)
+    for kj in range(8):
+        mg[kj % 4, kj // 4, :, 1792:1856] = gram[32 * kj:32 * kj + 16]
+        mg[kj % 4, kj // 4, :, 1856:1920] = gram[32 * kj + 16:32 * kj + 32]
+    for step in (1, 2, 3):
+        to = (yk + step) % 4
+        send(mg.at[to], rg.at[yk], rg_sem.at[yk], ((xl * 4 + to) * 8 + z, col))
+
     pass_x(4)
 
     pick = lax.broadcasted_iota(jnp.int32, (32, 256), 0)
@@ -183,10 +220,25 @@
     wanted = pick // 4 * 32 + pick // 2 % 2 * 16 + 2 * z + pick % 2
     r4[col] = jnp.dot(keep(source == wanted), sp[2:10].reshape(256, YX), preferred_element_type=F32).astype(BF)
     others(r4.at[col], r4_sem.at[col])
-    others(gc.at[col], gc_sem.at[col])
-    pass_g(6, 1)
-    pass_g(2, 7)
+
+    gi[...] = jnp.dot(wg[...], gp[...], preferred_element_type=F32).reshape(4, 32, YX)
+    send(gi.at[core], rgi.at[0], gi_sem.at[0], (gz, core))
+    send(gi.at[diag], rgi.at[1], gi_sem.at[1], (gz, core))
     hand_over(r4.at[far], r4_sem.at[far])
+    for buf, sem, slot, edge in ((sp, sp_sem, 0, 0), (sp, sp_sem, 1, 0), (sp, sp_sem, 10, 7), (sp, sp_sem, 11, 7)):
+        arrived(buf.at[slot], sem.at[slot])
+
+        @pl.when(k == edge)
+        def _():
+            buf[slot] = jnp.zeros(buf.shape[1:], BF)
+
+    for side in (0, 2):
+        xc[col, side] = sp[1 + z + side]
+        others(xc.at[col, side], xc_sem.at[col, side])
+
+    arrived(rgi.at[1], gi_sem.at[1])
+    up[...] = gi[far] + rgi[1]
+    send(up, rgi.at[2], gi_sem.at[2], (gz, far))
     arrived(r4.at[core], r4_sem.at[core])
     arrived(r4.at[diag], r4_sem.at[diag])
     rp[...] = jnp.dot(
@@ -211,10 +263,6 @@
             for ty, plane in enumerate(variants(line, SIDE, row, SIDE)):
                 at = (ty * 7 + tx) * 16
                 rv[at:at + 16, :] = plane
-        for b in range(3):
-            for e in range(3):
-                at = ((3 - b) * 7 + 3 - e) * 16
-                r9[v, (3 * b + e) * 16:(3 * b + e) * 16 + 16, :] = rv[at:at + 16, :]
         beside = sp[pl.ds(v, 5)].reshape(160, YX)
         flag = jnp.where(v == edge_plane, 1.0, 0.0).astype(BF)
         columns = jnp.concatenate([beside, sp[v + 2] * flag], axis=0)
@@ -222,33 +270,16 @@
         da[...] += part[:, 0:128]
         db[0:784, 0:64] += part[:, 128:192]
 
-    @pl.loop(2, 4)
+    @pl.loop(0, 8)
     def _(v):
         factor_plane(v)
 
-    pass_g(5, 1)
-    pass_g(3)
-
-    @pl.loop(4, 6)
-    def _(v):
-        factor_plane(v)
-
-    pass_g(4)
-    hand_over(gc.at[far], gc_sem.at[far])
-    for buf, sem, slot, edge in ((sp, sp_sem, 0, 0), (sp, sp_sem, 1, 0), (sp, sp_sem, 10, 7), (sp, sp_sem, 11, 7)):
-        arrived(buf.at[slot], sem.at[slot])
-
-        @pl.when(k == edge)
-        def _():
-            buf[slot] = jnp.zeros(buf.shape[1:], BF)
-
-    for side in (0, 2):
-        xc[col, side] = sp[1 + z + side]
-        others(xc.at[col, side], xc_sem.at[col, side])
-
-    @pl.loop(6, 10)
-    def _(v):
-        factor_plane(v % 8)
+    for step in (1, 2, 3):
+        slot = (yk + step) % 4
+        arrived(rg.at[slot], rg_sem.at[slot])
+    mx[1] = mg[yk, 1 - xl] + rg[(yk + 1) % 4, 1 - xl] + rg[(yk + 2) % 4, 1 - xl] + rg[(yk + 3) % 4, 1 - xl]
+    send(mx.at[1], rx, rx_sem.at[0], (((1 - xl) * 4 + yk) * 8 + z, col))
+    mx[0] = mg[yk, xl] + rg[(yk + 1) % 4, xl] + rg[(yk + 2) % 4, xl] + rg[(yk + 3) % 4, xl]
 
     lane = lax.broadcasted_iota(jnp.int32, (25, 128), 1)
 
@@ -282,56 +313,20 @@
                 copy.start()
             re[owner // 7] = me[owner]
 
-    for slot, edge in ((0, 0), (9, 7)):
-        arrived(gs.at[slot], gs_sem.at[slot])
-
-        @pl.when(k == edge)
-        def _():
-            gs[slot] = jnp.zeros((64, YX), BF)
-
-    cotangent_taps(0, gs[2 + z])
-    cotangent_taps(2, gs[z])
-    gi[...] = jnp.dot(wg[...], gp[...], preferred_element_type=F32).reshape(4, 32, YX)
-    send(gi.at[core], rgi.at[0], gi_sem.at[0], (gz, core))
-    send(gi.at[diag], rgi.at[1], gi_sem.at[1], (gz, core))
-
-    ga[...] = jnp.zeros((144, 128), F32)
-    gb[...] = jnp.zeros((144, 128), F32)
-
-    @pl.loop(0, 8)
-    def _(v):
-        part = lax.dot_general(
-            r9[v], gs[pl.ds(v, 3)].reshape(192, YX), NT, preferred_element_type=F32)
-        ga[...] += part[:, 0:128]
-        gb[:, 0:64] += part[:, 128:192]
-
-    wide_lane = lax.broadcasted_iota(jnp.int32, (9, 128), 1)
-    for kj in range(8):
-        tails = []
-        for p in range(2):
-            mw[kj, 9 * p:9 * p + 9] = ga[pl.ds(2 * kj + p, 9, stride=16), :]
-            tails.append(gb[pl.ds(2 * kj + p, 9, stride=16), :])
-        mw[kj, 18:27] = jnp.where(wide_lane < 64, tails[0], pltpu.roll(tails[1], shift=64, axis=1))
-    for kj in peers:
-        send(mw.at[kj], rw.at[k], rw_sem.at[k], (kj * 8 + z, col))
-
-    arrived(gc.at[core], gc_sem.at[core])
-    arrived(gc.at[diag], gc_sem.at[diag])
-    gram = lax.dot_general(gc[...].reshape(256, YX), g_ref[...], NT, preferred_element_type=F32)
-    for kj in range(8):
-        mg[kj, :, 0:64] = gram[32 * kj:32 * kj + 16]
-        mg[kj, :, 64:128] = gram[32 * kj + 16:32 * kj + 32]
-    for kj in peers:
-        send(mg.at[kj], rg.at[k], rg_sem.at[k], (kj * 8 + z, col))
-
-    arrived(rgi.at[1], gi_sem.at[1])
-    up[...] = gi[far] + rgi[1]
-    send(up, rgi.at[2], gi_sem.at[2], (gz, far))
+    arrived(rx, rx_sem.at[0])
+    total = mx[0] + rx[...]
+    for j in range(14):
+        for zj in range(8):
+            b3[zj, 2 * j:2 * j + 2, :] = total[2 * zj:2 * zj + 2, 128 * j:128 * j + 128]
+    sides = (total[:, 1792:1920], pltpu.roll(total[:, 1792:1920], shift=64, axis=1))
+    for zj in range(8):
+        b3[zj, 28:32, :] = sides[zj // 4][4 * (zj % 4):4 * (zj % 4) + 4]
+    for zj in ring:
+        send(b3.at[zj], rb.at[z], rb_sem.at[z], (k * 8 + zj, col))
+
     for side in (0, 2):
         hand_over(xc.at[far, side], xc_sem.at[far, side])
 
-    arrived(xc.at[core, 1], xc_sem.at[core, 1])
-    arrived(xc.at[diag, 1], xc_sem.at[diag, 1])
     for side in (0, 2):
         arrived(xc.at[core, side], xc_sem.at[core, side])
         arrived(xc.at[diag, side], xc_sem.at[diag, side])
@@ -344,16 +339,6 @@
                 tap = 9 * a + 3 * b + e
                 xp[tap * 128:(tap + 1) * 128, :] = shifted(line, b - 1, 0)
     y_ref[0] = jnp.dot(wy[...], xp[...], preferred_element_type=F32).astype(BF)
-
-    total = mg[k]
-    for kj in peers:
-        arrived(rg.at[kj], rg_sem.at[kj])
-        total = total + rg[kj]
-    halves = (total, pltpu.roll(total, shift=64, axis=1))
-    for zj in range(8):
-        b3[zj] = halves[zj // 4][4 * (zj % 4):4 * (zj % 4) + 4]
-    for zj in ring:
-        send(b3.at[zj], rb.at[z], rb_sem.at[z], (k * 8 + zj, col))
 
     arrived(rgi.at[0], gi_sem.at[0])
     arrived(rgi.at[2], gi_sem.at[2])
@@ -394,23 +379,17 @@
     for block in range(6):
         pf_ref[block * 9:block * 9 + 9, :] = factor[block * 16:block * 16 + 9]
 
-    total = mw[k]
-    for kj in peers:
-        arrived(rw.at[kj], rw_sem.at[kj])
-        total = total + rw[kj]
-    total = total * (1.0 / 256)
-    for p in range(2):
-        gw_ref[p * 27:p * 27 + 9, :] = total[18:27, 64 * p:64 * p + 64]
-        gw_ref[p * 27 + 9:p * 27 + 18, :] = total[9 * p:9 * p + 9, 64:128]
-        gw_ref[p * 27 + 18:p * 27 + 27, :] = total[9 * p:9 * p + 9, 0:64]
-
     total = b3[z]
     for zj in ring:
         arrived(rb.at[zj], rb_sem.at[zj])
         total = total + rb[zj]
-    gf_ref[...] = total[:, 0:64] * (1.0 / 65536)
-
-    for _, copy in x_edges + g_edges:
+    gf_ref[...] = total[28:32, 0:64] * (1.0 / 65536)
+    for tap in range(TAPS):
+        for p in range(2):
+            at = 2 * (tap // 2) + p
+            gw_ref[p * 27 + tap:p * 27 + tap + 1, :] = total[at:at + 1, 64 * (tap % 2):64 * (tap % 2) + 64] * (1.0 / 256)
+
+    for _, copy in x_edges:
         copy.wait_send()
     for copy in sends:
         copy.wait_send()
@@ -421,19 +400,25 @@
                 copy.wait_send()
 
 
+def deliver(*refs):
+    for i in range(5):
+        refs[5 + i][...] = refs[i][...]
+
+
 def shards(x_field, weights, grad_out):
     vmem = pl.BlockSpec(memory_space=pltpu.VMEM)
     there = pl.BlockSpec(memory_space=pl.ANY)
     dma = pltpu.SemaphoreType.DMA
-    return pl.pallas_call(
+    shapes = (
+        jax.ShapeDtypeStruct((1, 64, YX), BF),
+        jax.ShapeDtypeStruct((1, 32, YX), BF),
+        jax.ShapeDtypeStruct((54, 64), F32),
+        jax.ShapeDtypeStruct((54, 864), F32),
+        jax.ShapeDtypeStruct((4, 64), F32),
+    )
+    results = pl.pallas_call(
         kernel,
-        out_shape=(
-            jax.ShapeDtypeStruct((1, 64, YX), BF),
-            jax.ShapeDtypeStruct((1, 32, YX), BF),
-            jax.ShapeDtypeStruct((54, 64), F32),
-            jax.ShapeDtypeStruct((54, 864), F32),
-            jax.ShapeDtypeStruct((4, 64), F32),
-        ),
+        out_shape=shapes,
         in_specs=[there] * 5,
         out_specs=(vmem,) * 5,
         scratch_shapes=[
@@ -447,26 +432,23 @@
             pltpu.VMEM((128, 1728), BF),
             pltpu.VMEM((4, 3, 32, YX), BF),
             pltpu.VMEM((4, 64, YX), BF),
-            pltpu.VMEM((10, 64, YX), BF),
+            pltpu.VMEM((2, 64, YX), BF),
             pltpu.VMEM((12, 32, YX), BF),
             pltpu.VMEM((4, 32, YX), BF),
             pltpu.VMEM((8, 16, YX), BF),
-            pltpu.VMEM((8, 144, YX), BF),
             pltpu.VMEM((3456, YX), BF),
             pltpu.VMEM((1728, YX), BF),
             pltpu.VMEM((784, YX), BF),
             pltpu.VMEM((784, 128), F32),
             pltpu.VMEM((800, 128), F32),
-            pltpu.VMEM((144, 128), F32),
-            pltpu.VMEM((144, 128), F32),
-            pltpu.VMEM((8, 16, 128), F32),
-            pltpu.VMEM((8, 16, 128), F32),
-            pltpu.VMEM((8, 4, 128), F32),
-            pltpu.VMEM((8, 4, 128), F32),
+            pltpu.VMEM((4, 2, 16, 1920), F32),
+            pltpu.VMEM((4, 2, 16, 1920), F32),
+            pltpu.VMEM((2, 16, 1920), F32),
+            pltpu.VMEM((16, 1920), F32),
+            pltpu.VMEM((8, 32, 128), F32),
+            pltpu.VMEM((8, 32, 128), F32),
             pltpu.VMEM((8, 123, 128), F32),
             pltpu.VMEM((8, 123, 128), F32),
-            pltpu.VMEM((8, 27, 128), F32),
-            pltpu.VMEM((8, 27, 128), F32),
             pltpu.VMEM((8, 25, 128), F32),
             pltpu.VMEM((2, 25, 128), F32),
             pltpu.VMEM((4, 32, YX), F32),
@@ -478,11 +460,11 @@
             dma((8,)),
             dma((4, 3)),
             dma((4,)),
-            dma((10,)),
+            dma((2,)),
             dma((12,)),
             dma((4,)),
-            dma((8,)),
-            dma((8,)),
+            dma((4,)),
+            dma((1,)),
             dma((8,)),
             dma((8,)),
             dma((2,)),
@@ -492,6 +474,12 @@
             collective_id=0, has_side_effects=True, vmem_limit_bytes=56 * 2**20),
     )(x_field, grad_out, weights,
       jnp.asarray(channel_order(), BF), jnp.asarray(type_choice(), BF))
+    return pl.pallas_call(
+        deliver,
+        out_shape=shapes,
+        in_specs=[vmem] * 5,
+        out_specs=(vmem,) * 5,
+    )(*results)
 
 
 def solution(mesh):

time: 64.8 us -> 57.1 us (0.88)
  the two profiles are of different devices: /device:TPU:1 before, /device:TPU:8 now
where the time goes in v3:
time: 57.1 us; the launch traced here: 57 us
  Pallas kernels  56.4 us (99%)
  between operations  0.64 us (1%)
    pallas_call x1, Pallas kernels, shards(): pl.pallas_call(kernel, out_shape=shapes, in_specs=[there] * 5, out_specs=...  54.6 us
    pallas_call x1, Pallas kernels, shards(): pl.pallas_call(deliver, out_shape=shapes, in_specs=[vmem] * 5, out_specs=...  1.8 us

profile of v3, /device:TPU:8, one launch (start us, length us, event | category | flops | bytes accessed | tf_op | source)
XLA Modules:
  0.0 57.0 jit_solution(2758314040801740972)
XLA Ops:
  0.6 54.6 %shard_map.92 = (bf16[1,64,1024]{2,1,0:T(8,128)(2,1)}, bf16[1,32,1024]{2,1,0:T(8,128)(2,1)}, f32[54,64]{1,0:T(8,128)}, f32[54,864]{1,0:T(8,128)}, f32[4,64]{1,0:T(4,128)}) custom-call(bf16[1,32,1024]{2,1,0:T(8,128)(2,1)} %x_hbm.1, bf16[1,64,1024]{2,1,0:T(8,128)(2,1)} %g_hbm.1, bf16[64,3456]{1,0:T(8,128)(2,1)} %w_hbm.1, ...), custom_call_target="tpu_custom_call" | custom-call | tf_op jit(solution)/shard_map/pallas_call | solution.py:419
  55.2 1.8 %shard_map.93 = (bf16[1,64,1024]{2,1,0:T(8,128)(2,1)}, bf16[1,32,1024]{2,1,0:T(8,128)(2,1)}, f32[54,64]{1,0:T(8,128)}, f32[54,864]{1,0:T(8,128)}, f32[4,64]{1,0:T(4,128)}) custom-call(bf16[1,64,1024]{2,1,0:T(8,128)(2,1)} %get-tuple-element.10.refs_0_, bf16[1,32,1024]{2,1,0:T(8,128)(2,1)} %get-tuple-element.11.refs_1_, f32[54,64]{1,0:T(8,128)} %get-tuple-element.12.refs_2_, ...), custom_call_target="tpu_custom_call" | custom-call | tf_op jit(solution)/shard_map/pallas_call | solution.py:477

commit v4 on v3

--- a/solution.py
+++ b/solution.py
@@ -54,8 +54,8 @@
 def kernel(x_hbm, g_hbm, w_hbm, order_hbm, choice_hbm,
            y_ref, gi_ref, gw_ref, pf_ref, gf_ref,
            g_ref, w_ref, order_ref, choice_ref, column_ref, wt, wy, wg,
-           xc, gc, gh, sp, r4, rp, xp, gp, rv, da, db, mg, rg, mx, rx, b3, rb, mp, rpf, me, re, gi, rgi, up, lh,
-           send_sem, late_sem, load_sem, xc_sem, gc_sem, gh_sem, sp_sem, r4_sem, rg_sem, rx_sem, rb_sem, rpf_sem, re_sem,
+           xc, gc, gh, sp, r4, rp, xp, gp, rv, da, db, mg, rg, mx, rx, ng, nx, nt, ny, b3, rb, mp, rpf, me, re, gi, rgi, up, lh,
+           send_sem, late_sem, load_sem, xc_sem, gc_sem, gh_sem, sp_sem, r4_sem, rg_sem, rx_sem, nx_sem, ny_sem, rb_sem, rpf_sem, re_sem,
            gi_sem):
     gz, col = lax.axis_index("gz"), lax.axis_index("col")
     k, z = gz // 8, gz % 8
@@ -118,27 +118,37 @@
         load.wait()
     pl.semaphore_wait(barrier, len(partners))
 
-    def edge_copies(buf, sem, base, edges):
-        return [(plane, pltpu.make_async_remote_copy(
-            src_ref=buf.at[base + plane], dst_ref=buf.at[home], send_sem=late_sem.at[late], recv_sem=sem.at[home],
-            device_id=((k + step) % 8 * 8 + z, col), device_id_type=MESH)) for plane, home, step, late in edges]
-
-    x_edges = edge_copies(sp, sp_sem, 2, ((0, 10, 7, 0), (1, 11, 7, 1), (6, 0, 1, 2), (7, 1, 1, 3)))
-
-    def pass_on(buf, sem, base, edges, offset, steps):
-        at = (z + offset) % 8
-        slot = base + at
-        if offset:
-            arrived(buf.at[slot], sem.at[slot])
-        for step in steps:
-            send(buf.at[slot], buf.at[slot], sem.at[slot], on_ring(step))
-        for plane, copy in edges:
-            @pl.when(at == plane)
-            def _():
-                copy.start()
-
-    def pass_x(offset, *steps):
-        pass_on(sp, sp_sem, 2, x_edges, offset, steps)
+    x_edges = [(plane, pltpu.make_async_remote_copy(
+        src_ref=sp.at[2 + plane], dst_ref=sp.at[home], send_sem=late_sem.at[late], recv_sem=sp_sem.at[home, 0],
+        device_id=((k + step) % 8 * 8 + z, col), device_id_type=MESH))
+        for late, (plane, home, step) in enumerate(((0, 10, 7), (1, 11, 7), (6, 0, 1), (7, 1, 1)))]
+
+    def half(offset, part):
+        slot = 2 + (z + offset) % 8
+        return sp.at[slot, pl.ds(16 * part, 16)], sp_sem.at[slot, part]
+
+    def take(offset, part):
+        arrived(*half(offset, part))
+
+    def give(offset, part, step):
+        rows, sem = half(offset, part)
+        send(rows, rows, sem, on_ring(step))
+
+    def pass_on(up, down):
+        for part in (0, 1):
+            if up:
+                take(up, part)
+            give(up, part, 1)
+            if down:
+                take(down, 1 - part)
+            give(down, 1 - part, 7)
+
+    def outward(*offsets):
+        for offset in offsets:
+            for plane, copy in x_edges:
+                @pl.when((z + offset) % 8 == plane)
+                def _():
+                    copy.start()
 
     def others(buf, sem):
         send(buf, buf, sem, (gz, far))
@@ -148,14 +158,8 @@
         arrived(buf, sem)
         send(buf, buf, sem, (gz, core))
 
-    def halves(buf, sem, base):
-        rows = buf.shape[1] // 2
-        for offset, step, first in ((5, 1, 0), (3, 7, rows)):
-            slot = base + (z + offset) % 8
-            part = buf.at[slot, pl.ds(first, rows)]
-            send(part, part, sem.at[slot], on_ring(step))
-
-    pass_x(0, 1, 7)
+    pass_on(0, 0)
+    outward(0)
     for load in other_loads:
         load.wait()
     send(g_ref, gh.at[0], gh_sem.at[0], (above, col))
@@ -171,8 +175,58 @@
         wg[:, tap * 64:tap * 64 + 64] = block[:, 0:64].astype(BF)
         wy[:, tap * 128:tap * 128 + 128] = jnp.transpose(block)[0:64].astype(BF)
 
-    pass_x(7, 1)
-    pass_x(1, 7)
+    pass_on(7, 1)
+    outward(7, 1)
+
+    cotangent_taps(1, g_ref[...])
+    pass_on(6, 2)
+    outward(6, 2)
+    hand_over(xc.at[far, 1], xc_sem.at[far, 1])
+    for slot, edge in ((0, 0), (1, 63)):
+        arrived(gh.at[slot], gh_sem.at[slot])
+
+        @pl.when(gz == edge)
+        def _():
+            gh[slot] = jnp.zeros((64, YX), BF)
+
+    cotangent_taps(0, gh[1])
+    cotangent_taps(2, gh[0])
+    take(5, 0)
+    give(5, 0, 1)
+    take(3, 1)
+    give(3, 1, 7)
+    take(5, 1)
+    take(3, 0)
+    outward(5, 3)
+    arrived(xc.at[core, 1], xc_sem.at[core, 1])
+    arrived(xc.at[diag, 1], xc_sem.at[diag, 1])
+    grad_w = lax.dot_general(xc[:, 1].reshape(128, YX), gp[...], NT, preferred_element_type=F32)
+    take(4, 0)
+    take(4, 1)
+    outward(4)
+
+    pick = lax.broadcasted_iota(jnp.int32, (32, 256), 0)
+    source = lax.broadcasted_iota(jnp.int32, (32, 256), 1)
+    wanted = pick // 4 * 32 + pick // 2 % 2 * 16 + 2 * z + pick % 2
+    r4[col] = jnp.dot(keep(source == wanted), sp[2:10].reshape(256, YX), preferred_element_type=F32).astype(BF)
+    others(r4.at[col], r4_sem.at[col])
+    hand_over(gc.at[far], gc_sem.at[far])
+
+    for kj in range(8):
+        mg[kj % 4, kj // 4] = grad_w[16 * kj:16 * kj + 16, 0:1280]
+        ng[kj // 4, kj % 4, :, 0:448] = grad_w[16 * kj:16 * kj + 16, 1280:1728]
+        ng[kj // 4, kj % 4, :, 448:512] = jnp.zeros((16, 64), F32)
+    arrived(gc.at[core], gc_sem.at[core])
+    arrived(gc.at[diag], gc_sem.at[diag])
+    gram = lax.dot_general(gc[...].reshape(256, YX), g_ref[...], NT, preferred_element_type=F32)
+    for kj in range(8):
+        ng[kj // 4, kj % 4, :, 512:576] = gram[32 * kj:32 * kj + 16]
+        ng[kj // 4, kj % 4, :, 576:640] = gram[32 * kj + 16:32 * kj + 32]
+    send(ng.at[1 - xl], nx, nx_sem.at[0], (((1 - xl) * 4 + yk) * 8 + z, col))
+    for step in (1, 2, 3):
+        to = (yk + step) % 4
+        send(mg.at[to], rg.at[yk], rg_sem.at[yk], ((xl * 4 + to) * 8 + z, col))
+
 
     entry = lax.broadcasted_iota(jnp.int32, (128, 864), 0)
     column = lax.broadcasted_iota(jnp.int32, (128, 864), 1)
@@ -180,57 +234,16 @@
     for be in range(9):
         column_ref[be * 128:be * 128 + 128, :] = keep(column == home + be)
 
-    cotangent_taps(1, g_ref[...])
-    pass_x(6, 1)
-    pass_x(2, 7)
-    hand_over(xc.at[far, 1], xc_sem.at[far, 1])
-    hand_over(gc.at[far], gc_sem.at[far])
-    pass_x(5)
-    pass_x(3)
-    halves(sp, sp_sem, 2)
-    for slot, edge in ((0, 0), (1, 63)):
-        arrived(gh.at[slot], gh_sem.at[slot])
-
-        @pl.when(gz == edge)
-        def _():
-            gh[slot] = jnp.zeros((64, YX), BF)
-
-    cotangent_taps(0, gh[1])
-    cotangent_taps(2, gh[0])
-    arrived(xc.at[core, 1], xc_sem.at[core, 1])
-    arrived(xc.at[diag, 1], xc_sem.at[diag, 1])
-    grad_w = lax.dot_general(xc[:, 1].reshape(128, YX), gp[...], NT, preferred_element_type=F32)
-    for kj in range(8):
-        mg[kj % 4, kj // 4, :, 0:1728] = grad_w[16 * kj:16 * kj + 16]
-        mg[kj % 4, kj // 4, :, 1728:1792] = jnp.zeros((16, 64), F32)
-    arrived(gc.at[core], gc_sem.at[core])
-    arrived(gc.at[diag], gc_sem.at[diag])
-    gram = lax.dot_general(gc[...].reshape(256, YX), g_ref[...], NT, preferred_element_type=F32)
-    for kj in range(8):
-        mg[kj % 4, kj // 4, :, 1792:1856] = gram[32 * kj:32 * kj + 16]
-        mg[kj % 4, kj // 4, :, 1856:1920] = gram[32 * kj + 16:32 * kj + 32]
-    for step in (1, 2, 3):
-        to = (yk + step) % 4
-        send(mg.at[to], rg.at[yk], rg_sem.at[yk], ((xl * 4 + to) * 8 + z, col))
-
-    pass_x(4)
-
-    pick = lax.broadcasted_iota(jnp.int32, (32, 256), 0)
-    source = lax.broadcasted_iota(jnp.int32, (32, 256), 1)
-    wanted = pick // 4 * 32 + pick // 2 % 2 * 16 + 2 * z + pick % 2
-    r4[col] = jnp.dot(keep(source == wanted), sp[2:10].reshape(256, YX), preferred_element_type=F32).astype(BF)
-    others(r4.at[col], r4_sem.at[col])
-
     gi[...] = jnp.dot(wg[...], gp[...], preferred_element_type=F32).reshape(4, 32, YX)
     send(gi.at[core], rgi.at[0], gi_sem.at[0], (gz, core))
     send(gi.at[diag], rgi.at[1], gi_sem.at[1], (gz, core))
     hand_over(r4.at[far], r4_sem.at[far])
-    for buf, sem, slot, edge in ((sp, sp_sem, 0, 0), (sp, sp_sem, 1, 0), (sp, sp_sem, 10, 7), (sp, sp_sem, 11, 7)):
-        arrived(buf.at[slot], sem.at[slot])
+    for slot, edge in ((0, 0), (1, 0), (10, 7), (11, 7)):
+        arrived(sp.at[slot], sp_sem.at[slot, 0])
 
         @pl.when(k == edge)
         def _():
-            buf[slot] = jnp.zeros(buf.shape[1:], BF)
+            sp[slot] = jnp.zeros((32, YX), BF)
 
     for side in (0, 2):
         xc[col, side] = sp[1 + z + side]
@@ -270,7 +283,17 @@
         da[...] += part[:, 0:128]
         db[0:784, 0:64] += part[:, 128:192]
 
-    @pl.loop(0, 8)
+    @pl.loop(0, 5)
+    def _(v):
+        factor_plane(v)
+
+    arrived(nx, nx_sem.at[0])
+    nt[...] = ng[xl] + nx[...]
+    for step in (1, 2, 3):
+        to = (yk + step) % 4
+        send(nt.at[to], ny.at[yk], ny_sem.at[yk], ((xl * 4 + to) * 8 + z, col))
+
+    @pl.loop(5, 8)
     def _(v):
         factor_plane(v)
 
@@ -314,11 +337,17 @@
             re[owner // 7] = me[owner]
 
     arrived(rx, rx_sem.at[0])
-    total = mx[0] + rx[...]
+    early = mx[0] + rx[...]
+    late = nt[yk]
+    for step in (1, 2, 3):
+        slot = (yk + step) % 4
+        arrived(ny.at[slot], ny_sem.at[slot])
+        late = late + ny[slot]
+    tiles = [early[:, 128 * j:128 * j + 128] for j in range(10)] + [late[:, 128 * j:128 * j + 128] for j in range(5)]
     for j in range(14):
         for zj in range(8):
-            b3[zj, 2 * j:2 * j + 2, :] = total[2 * zj:2 * zj + 2, 128 * j:128 * j + 128]
-    sides = (total[:, 1792:1920], pltpu.roll(total[:, 1792:1920], shift=64, axis=1))
+            b3[zj, 2 * j:2 * j + 2, :] = tiles[j][2 * zj:2 * zj + 2]
+    sides = (tiles[14], pltpu.roll(tiles[14], shift=64, axis=1))
     for zj in range(8):
         b3[zj, 28:32, :] = sides[zj // 4][4 * (zj % 4):4 * (zj % 4) + 4]
     for zj in ring:
@@ -441,10 +470,14 @@
             pltpu.VMEM((784, YX), BF),
             pltpu.VMEM((784, 128), F32),
             pltpu.VMEM((800, 128), F32),
-            pltpu.VMEM((4, 2, 16, 1920), F32),
-            pltpu.VMEM((4, 2, 16, 1920), F32),
-            pltpu.VMEM((2, 16, 1920), F32),
-            pltpu.VMEM((16, 1920), F32),
+            pltpu.VMEM((4, 2, 16, 1280), F32),
+            pltpu.VMEM((4, 2, 16, 1280), F32),
+            pltpu.VMEM((2, 16, 1280), F32),
+            pltpu.VMEM((16, 1280), F32),
+            pltpu.VMEM((2, 4, 16, 640), F32),
+            pltpu.VMEM((4, 16, 640), F32),
+            pltpu.VMEM((4, 16, 640), F32),
+            pltpu.VMEM((4, 16, 640), F32),
             pltpu.VMEM((8, 32, 128), F32),
             pltpu.VMEM((8, 32, 128), F32),
             pltpu.VMEM((8, 123, 128), F32),
@@ -461,10 +494,12 @@
             dma((4, 3)),
             dma((4,)),
             dma((2,)),
-            dma((12,)),
+            dma((12, 2)),
             dma((4,)),
             dma((4,)),
             dma((1,)),
+            dma((1,)),
+            dma((4,)),
             dma((8,)),
             dma((8,)),
             dma((2,)),

time: 57.1 us -> 52.1 us (0.912)
  the two profiles are of different devices: /device:TPU:8 before, /device:TPU:1 now
where the time goes in v4:
time: 52.1 us; the launch traced here: 52 us
  Pallas kernels  51.4 us (99%)
  between operations  0.64 us (1%)
    pallas_call x1, Pallas kernels, shards(): pl.pallas_call(kernel, out_shape=shapes, in_specs=[there] * 5, out_specs=...  49.6 us
    pallas_call x1, Pallas kernels, shards(): pl.pallas_call(deliver, out_shape=shapes, in_specs=[vmem] * 5, out_specs=...  1.8 us

profile of v4, /device:TPU:1, one launch (start us, length us, event | category | flops | bytes accessed | tf_op | source)
XLA Modules:
  0.0 52.0 jit_solution(15735662935804793290)
XLA Ops:
  0.6 49.6 %shard_map.92 = (bf16[1,64,1024]{2,1,0:T(8,128)(2,1)}, bf16[1,32,1024]{2,1,0:T(8,128)(2,1)}, f32[54,64]{1,0:T(8,128)}, f32[54,864]{1,0:T(8,128)}, f32[4,64]{1,0:T(4,128)}) custom-call(bf16[1,32,1024]{2,1,0:T(8,128)(2,1)} %x_hbm.1, bf16[1,64,1024]{2,1,0:T(8,128)(2,1)} %g_hbm.1, bf16[64,3456]{1,0:T(8,128)(2,1)} %w_hbm.1, ...), custom_call_target="tpu_custom_call" | custom-call | tf_op jit(solution)/shard_map/pallas_call | solution.py:448
  50.2 1.8 %shard_map.93 = (bf16[1,64,1024]{2,1,0:T(8,128)(2,1)}, bf16[1,32,1024]{2,1,0:T(8,128)(2,1)}, f32[54,64]{1,0:T(8,128)}, f32[54,864]{1,0:T(8,128)}, f32[4,64]{1,0:T(4,128)}) custom-call(bf16[1,64,1024]{2,1,0:T(8,128)(2,1)} %get-tuple-element.10.refs_0_, bf16[1,32,1024]{2,1,0:T(8,128)(2,1)} %get-tuple-element.11.refs_1_, f32[54,64]{1,0:T(8,128)} %get-tuple-element.12.refs_2_, ...), custom_call_target="tpu_custom_call" | custom-call | tf_op jit(solution)/shard_map/pallas_call | solution.py:512

commit v5 on v4

--- a/solution.py
+++ b/solution.py
@@ -283,7 +283,7 @@
         da[...] += part[:, 0:128]
         db[0:784, 0:64] += part[:, 128:192]
 
-    @pl.loop(0, 5)
+    @pl.loop(0, 4)
     def _(v):
         factor_plane(v)
 
@@ -293,7 +293,7 @@
         to = (yk + step) % 4
         send(nt.at[to], ny.at[yk], ny_sem.at[yk], ((xl * 4 + to) * 8 + z, col))
 
-    @pl.loop(5, 8)
+    @pl.loop(4, 7)
     def _(v):
         factor_plane(v)
 
@@ -303,6 +303,11 @@
     mx[1] = mg[yk, 1 - xl] + rg[(yk + 1) % 4, 1 - xl] + rg[(yk + 2) % 4, 1 - xl] + rg[(yk + 3) % 4, 1 - xl]
     send(mx.at[1], rx, rx_sem.at[0], (((1 - xl) * 4 + yk) * 8 + z, col))
     mx[0] = mg[yk, xl] + rg[(yk + 1) % 4, xl] + rg[(yk + 2) % 4, xl] + rg[(yk + 3) % 4, xl]
+
+
+    @pl.loop(7, 8)
+    def _(v):
+        factor_plane(v)
 
     lane = lax.broadcasted_iota(jnp.int32, (25, 128), 1)
 

time: 52.1 us -> 51.7 us (level)
  no operation moved by 1% of the time
where the time goes in v5:
time: 51.7 us; the launch traced here: 51.6 us
  Pallas kernels  50.9 us (98%)
  between operations  0.64 us (1%)
    pallas_call x1, Pallas kernels, shards(): pl.pallas_call(kernel, out_shape=shapes, in_specs=[there] * 5, out_specs=...  49.1 us
    pallas_call x1, Pallas kernels, shards(): pl.pallas_call(deliver, out_shape=shapes, in_specs=[vmem] * 5, out_specs=...  1.8 us

profile of v5, /device:TPU:1, one launch (start us, length us, event | category | flops | bytes accessed | tf_op | source)
XLA Modules:
  0.0 51.6 jit_solution(41734644790120231)
XLA Ops:
  0.6 49.1 %shard_map.92 = (bf16[1,64,1024]{2,1,0:T(8,128)(2,1)}, bf16[1,32,1024]{2,1,0:T(8,128)(2,1)}, f32[54,64]{1,0:T(8,128)}, f32[54,864]{1,0:T(8,128)}, f32[4,64]{1,0:T(4,128)}) custom-call(bf16[1,32,1024]{2,1,0:T(8,128)(2,1)} %x_hbm.1, bf16[1,64,1024]{2,1,0:T(8,128)(2,1)} %g_hbm.1, bf16[64,3456]{1,0:T(8,128)(2,1)} %w_hbm.1, ...), custom_call_target="tpu_custom_call" | custom-call | tf_op jit(solution)/shard_map/pallas_call | solution.py:453
  49.8 1.8 %shard_map.93 = (bf16[1,64,1024]{2,1,0:T(8,128)(2,1)}, bf16[1,32,1024]{2,1,0:T(8,128)(2,1)}, f32[54,64]{1,0:T(8,128)}, f32[54,864]{1,0:T(8,128)}, f32[4,64]{1,0:T(4,128)}) custom-call(bf16[1,64,1024]{2,1,0:T(8,128)(2,1)} %get-tuple-element.10.refs_0_, bf16[1,32,1024]{2,1,0:T(8,128)(2,1)} %get-tuple-element.11.refs_1_, f32[54,64]{1,0:T(8,128)} %get-tuple-element.12.refs_2_, ...), custom_call_target="tpu_custom_call" | custom-call | tf_op jit(solution)/shard_map/pallas_call | solution.py:517
